TPU v7x, 512 devices: a whole 4x8x8 slice. The times are simulated.
512 devices in a mesh: row: 16 (over z_lo, x), col: 8 (over y), vir: 4 (over z_hi, core).
Axes of the slice: x: 4, y: 8, z: 8 (z_hi: 2, z_lo: 4; z = z_hi * 4 + z_lo), core: 2. Of those that a mesh axis runs over, the one named last changes fastest.
Arguments:
- amplitudes: bfloat16 [8, 16, 1, 8, 16, 3, 1792], P(None, 'row', None, 'col'), may hold values from -6 to 6
- integrals: bfloat16 [64, 64, 3, 1792], P('vir', 'row', None, 'col'), may hold values from -0.25 to 0.25
- hole_integrals: bfloat16 [128, 1, 8, 16, 3, 64], P(None, None, 'col'), may hold values from -0.3125 to 0.3125
- irreps: int32 [112], replicated, may hold values from 0 to 7
- occ_energy: float32 [128], replicated, may hold values from -2 to -0.5
- vir_energy: float32 [64], replicated, may hold values from 0.5 to 3
Outputs:
- increment: bfloat16 [8, 16, 1, 8, 16, 64, 64], P(None, 'row', None, 'col', None, 'vir')
All inputs are finite; a program needn't handle non-finite values.
Results may differ from a plain program's by a relative error of at most 0.001.
Values may be sent and summed in bfloat16 or wider, within the bound.
A program may use at most 128 MiB of HBM per device.

v0:
```python
import jax
import jax.numpy as jnp
from jax import lax
from jax.sharding import PartitionSpec as P

NO = 128
NV = 1792
SA = 64
CW = 3
VBLK = 16


def masked_block(piece, lab_a, lab_b, lab_c, lab_d):
    left = jnp.bitwise_xor(lab_a[:, None], lab_b[None, :])
    right = jnp.bitwise_xor(lab_c[:, None], lab_d[None, :])
    keep = left[:, :, None, None] == right[None, None, :, :]
    return jnp.where(keep, piece, jnp.zeros_like(piece))


def contract(amp_rows, block):
    return lax.dot_general(
        amp_rows, block, (((1, 2), (2, 3)), ((), ())), preferred_element_type=jnp.float32
    )


def local(amplitudes, integrals, hole_integrals, irreps, occ_energy, vir_energy):
    vir_pos = lax.axis_index("vir")
    row_pos = lax.axis_index("row")
    col_pos = lax.axis_index("col")
    n_row = lax.axis_size("row")
    n_col = lax.axis_size("col")
    occ_a = amplitudes.shape[0]
    occ_h = amplitudes.shape[2]
    width_a = integrals.shape[0]
    pairs = occ_a * occ_h * n_row
    labels = jnp.repeat(irreps, VBLK)
    lab_a = lax.dynamic_slice_in_dim(labels, vir_pos * width_a, width_a)
    lab_c = labels[:CW]
    amp_rows = amplitudes.reshape(pairs, CW, NV)
    full_d = lax.all_gather(integrals, "col", axis=3, tiled=True)
    piece = lax.all_gather(full_d, "row", axis=1, tiled=True)
    lab_b = lax.slice_in_dim(labels, 0, piece.shape[1], axis=0)
    ladder = contract(amp_rows, masked_block(piece, lab_a, lab_b, lab_c, labels))
    slab_part = lax.dynamic_slice_in_dim(amplitudes, vir_pos * width_a, width_a, 6)
    every_k = lax.all_gather(slab_part, "col", axis=3, tiled=True).reshape(occ_a, NO, CW, width_a)
    hole_mat = hole_integrals.reshape(NO, occ_h * n_row, CW, SA)
    crossed = -lax.dot_general(
        every_k, hole_mat, (((1, 2), (0, 2)), ((), ())), preferred_element_type=jnp.float32
    )
    crossed = jnp.transpose(crossed, (0, 2, 1, 3)).reshape(pairs, width_a, SA)
    mixed = ladder + crossed
    groups = occ_a // n_col
    outgoing = mixed.reshape(groups, n_col, occ_h, n_row, width_a, SA)
    outgoing = jnp.transpose(outgoing, (3, 1, 0, 2, 4, 5)).reshape(
        n_row * n_col, groups, occ_h, width_a, SA
    )
    incoming = lax.all_to_all(
        lax.all_to_all(outgoing, ("row", "col"), split_axis=0, concat_axis=0, tiled=True),
        "vir",
        split_axis=4,
        concat_axis=3,
        tiled=True,
    )
    incoming = incoming.reshape(n_row, n_col, groups, occ_h, SA, width_a)
    mirrored = jnp.transpose(incoming, (3, 1, 2, 0, 5, 4)).reshape(pairs, width_a, SA)
    energy_i = lax.dynamic_slice_in_dim(occ_energy.reshape(occ_a, n_row), row_pos, 1, 1).reshape(
        occ_a
    )
    energy_j = lax.dynamic_slice_in_dim(
        occ_energy.reshape(occ_h, n_col, n_row), col_pos, 1, 1
    ).reshape(occ_h * n_row)
    energy_a = lax.dynamic_slice_in_dim(vir_energy, vir_pos * width_a, width_a)
    pair_sum = (energy_i[:, None] + energy_j[None, :]).reshape(pairs)
    denom = pair_sum[:, None, None] - energy_a[None, :, None] - vir_energy[None, None, :]
    result = ((mixed + mirrored) / denom).astype(jnp.bfloat16)
    return result.reshape(occ_a, 1, occ_h, 1, n_row, width_a, SA)


def solution(mesh):
    in_specs = (
        P(None, "row", None, "col", None, None, None),
        P("vir", "row", None, "col"),
        P(None, None, "col", None, None, None),
        P(),
        P(),
        P(),
    )
    out_specs = P(None, "row", None, "col", None, "vir", None)
    return jax.shard_map(local, mesh=mesh, in_specs=in_specs, out_specs=out_specs, check_vma=False)
```

profile of v0, /device:TPU:1, one launch (start us, length us, event | category | flops | bytes accessed | tf_op | source)
XLA Modules:
  0.0 290.0 jit_solution(2812510031302982527)
XLA Ops:
  6.5 1.5 copy.21
  8.0 0.0 copy-start.1
  8.0 54.8 %all_gather.9 = bf16[16,4,3,1792]{0,1,2,3:T(4,128)(2,1)} all-gather(bf16[16,4,3,224]{0,1,2,3:T(4,128)(2,1)S(1)} %copy.21), channel_id=1, replica_groups=mesh['row'=16,'col'=8,'vir'=4] {'col'}, dimensions={3}, use_global_device_ids=true | all-gather | bytes 774144 | tf_op jit(solution)/shard_map/all_gather | solution.py:40
  62.9 7.7 %copy.22 = bf16[16,4,3,1792]{3,0,2,1:T(8,128)(2,1)} copy(bf16[16,4,3,1792]{0,1,2,3:T(4,128)(2,1)} %all_gather.9) | data formatting | bytes 1376256 | tf_op jit(solution)/shard_map/all_gather | solution.py:40
  70.5 0.0 all-gather.2.cloned.1.call-update
  70.6 0.1 broadcast_in_dim.6
  70.7 0.1 reshape.146
  70.7 0.1 dynamic_slice.15
  70.8 0.1 broadcast_in_dim.7
  70.9 0.1 xor.37
  71.0 1.2 copy.23
  72.2 0.1 constant_dynamic-slice_fusion.1
  72.3 23.4 %all_gather.11 = bf16[8,1,1,8,16,3,16]{6,4,5,3,2,1,0:T(8,128)(2,1)S(1)} all-gather(bf16[8,1,1,1,16,3,16]{6,4,5,3,2,1,0:T(8,128)(2,1)S(1)} %constant_dynamic-slice_fusion.1), channel_id=1, replica_groups=mesh['row'=16,'col'=8,'vir'=4] {'col'}, dimensions={3}, use_global_device_ids=true | all-gather | bytes 110592 | tf_op jit(solution)/shard_map/all_gather | solution.py:45
  95.7 0.5 copy.25
  96.2 0.5 reshape.160
  96.7 0.6 fusion.4
  97.3 0.4 copy.26
  97.8 0.1 broadcast_xor_fusion
  97.8 0.1 broadcast_xor_fusion.1
  97.9 111.4 %all-gather.2.cloned.1.call-done = bf16[16,64,3,1792]{3,0,2,1:T(8,128)(2,1)} async-done(((bf16[16,4,3,1792]{3,0,2,1:T(8,128)(2,1)}), bf16[16,64,3,1792]{3,0,2,1:T(8,128)(2,1)}) %all-gather.2.cloned.1.call-update) | async-done | bytes 11010064 | tf_op jit(solution)/shard_map/all_gather | solution.py:41
  209.3 6.3 %fusion = f32[16,64,128,1]{2,0,3,1:T(8,128)S(1)} fusion(bf16[128,3,1792,1]{2,0,1,3:T(8,128)(2,1)} %bitcast.53, bf16[16,64,3,1792]{3,0,2,1:T(8,128)(2,1)} %all-gather.2.cloned.1.call-done, s32[3,1792]{1,0:T(4,128)S(1)} %broadcast_xor_fusion.1, s32[16,64]{0,1:T(8,128)S(1)} %broadcast_xor_fusion), kind=kOutput, calls=%fused_computation.1 | convolution fusion | flops 1420296192 | bytes 12936192 | tf_op jit(solution)/shard_map/dot_general | solution.py:21
  215.6 0.2 bitcast_add_fusion
  215.9 0.0 copy-start.3
  215.9 0.0 copy-start.4
  215.9 0.5 copy.27
  216.4 0.1 copy.28
  216.5 0.7 reshape.165
  217.2 28.9 %all_to_all.20 = f32[128,1,1024]{2,1,0:T(1,128)S(1)} all-to-all(f32[128,1,1024]{2,1,0:T(1,128)S(1)} %reshape.165), channel_id=1, replica_groups=mesh['row'=16,'col'=8,'vir'=4] {'row','col'}, dimensions={0} | all-to-all | bytes 1048576 | tf_op jit(solution)/shard_map/all_to_all | solution.py:58
  246.1 0.5 broadcast.65
  246.6 1.9 reduce.2
  248.5 0.3 reshape.166
  248.8 1.3 copy.30
  250.1 8.6 %all-to-all-start.1 = ((f32[128,1,1,16,64]{0,3,2,1,4:T(8,128)}), f32[128,1,1,16,64]{0,3,2,1,4:T(8,128)S(1)}, u32[]{:S(2)}, u32[]{:S(2)}) async-start(f32[128,1,1,16,64]{0,3,2,1,4:T(8,128)} %copy.30), calls=%async_computation.1 | async-start | bytes 1048576 | tf_op jit(solution)/shard_map/all_to_all | solution.py:57
  258.7 0.1 reshape.155
  258.7 0.1 reshape.156
  258.8 0.2 dynamic-slice_reduce_fusion
  259.0 0.1 broadcast_add_fusion
  259.1 0.1 add.53
  259.2 0.1 dynamic_slice.19
  259.3 0.1 broadcast_subtract_fusion
  259.3 13.6 %all-to-all-done.1 = f32[128,1,1,16,64]{0,3,2,1,4:T(8,128)S(1)} async-done(((f32[128,1,1,16,64]{0,3,2,1,4:T(8,128)}), f32[128,1,1,16,64]{0,3,2,1,4:T(8,128)S(1)}, u32[]{:S(2)}, u32[]{:S(2)}) %all-to-all-start.1) | async-done | bytes 524320 | tf_op jit(solution)/shard_map/all_to_all | solution.py:57
  273.0 0.2 copy.31
  273.1 4.4 %copy.32 = f32[128,1,1,4,16,16]{4,3,5,0,2,1:T(4,128)} copy(f32[128,1,1,4,16,16]{0,5,3,4,2,1:T(8,128)S(1)} %bitcast.52) | data formatting | bytes 1048576 | tf_op jit(solution)/shard_map/all_to_all | solution.py:57
  277.5 3.7 %reshape.153 = f32[16,8,1,1,64,16]{4,5,1,0,3,2:T(8,128)S(1)} reshape(f32[128,1,1,4,16,16]{4,3,5,0,2,1:T(4,128)} %copy.32) | data formatting | bytes 1048576 | tf_op jit(solution)/shard_map/reshape | solution.py:64
  281.2 0.1 copy.33
  281.3 0.4 copy.34
  281.8 0.2 divide_convert_fusion
  282.0 1.2 copy.35
  (10 shorter events, 0.0 us)
Async XLA Ops:
  6.5 90.2 %copy-start = (bf16[128,1,1,16,3,64]{0,5,4,3,2,1:T(8,128)(2,1)S(1)}, bf16[128,1,1,16,3,64]{0,5,4,3,2,1:T(8,128)(2,1)}, u32[]{:S(2)}) copy-start(bf16[128,1,1,16,3,64]{0,5,4,3,2,1:T(8,128)(2,1)} %param.8) | copy-start | bytes 2359300
  6.5 202.8 %all-gather.2.cloned.1.call-start = ((), (), s32[]{:S(2)}) async-start(), calls=%async_computation.2 | async-start | bytes 11698176 | tf_op jit(solution)/shard_map/all_gather | solution.py:41
  8.0 62.5 %copy-start.2 = (s32[112]{0:T(128)S(1)}, s32[112]{0:T(128)}, u32[]{:S(2)}) copy-start(s32[112]{0:T(128)} %param.9) | copy-start | bytes 1348
  8.0 63.0 %copy-start.1 = (bf16[8,1,1,1,16,3,1792]{6,4,5,3,2,1,0:T(8,128)(2,1)S(1)}, bf16[8,1,1,1,16,3,1792]{6,4,5,3,2,1,0:T(8,128)(2,1)}, u32[]{:S(2)}) copy-start(bf16[8,1,1,1,16,3,1792]{6,4,5,3,2,1,0:T(8,128)(2,1)} %param.6) | copy-start | bytes 4128772
  215.9 42.8 %copy-start.3 = (f32[128]{0:T(128)S(1)}, f32[128]{0:T(128)}, u32[]{:S(2)}) copy-start(f32[128]{0:T(128)} %param.10) | copy-start | bytes 1540
  215.9 43.3 %copy-start.4 = (f32[64]{0:T(128)S(1)}, f32[64]{0:T(128)}, u32[]{:S(2)}) copy-start(f32[64]{0:T(128)} %param.11) | copy-start | bytes 772
  250.1 22.9 %all-to-all-start.1 = ((f32[128,1,1,16,64]{0,3,2,1,4:T(8,128)}), f32[128,1,1,16,64]{0,3,2,1,4:T(8,128)S(1)}, u32[]{:S(2)}, u32[]{:S(2)}) async-start(f32[128,1,1,16,64]{0,3,2,1,4:T(8,128)} %copy.30), calls=%async_computation.1 | async-start | bytes 1048576 | tf_op jit(solution)/shard_map/all_to_all | solution.py:57
Sparse Core Ops, SparseCore 0:
  70.7 138.6 all-gather.1
where the time goes:
time: 290 us
  waiting for transfers between devices  125 us (43%)
  blocking collectives  107 us (37%)
  local copies, waits for them, and re-layouts  26.1 us (9%)
  between operations  13.6 us (5%)
  starting transfers between devices  8.58 us (3%)
  matrix products  6.9 us (2%)
    all_gather x1, waiting for transfers between devices, local(): piece = lax.all_gather(full_d, 'row', axis=1, tiled=True)  111 us
    all_gather x1, blocking collectives, local(): full_d = lax.all_gather(integrals, 'col', axis=3, tiled=True)  54.8 us
    all_to_all x1, blocking collectives, local(): lax.all_to_all(outgoing, ('row', 'col'), split_axis=0, concat_axis=0, til...  28.9 us
    all_gather x1, blocking collectives, local(): lax.all_gather(slab_part, 'col', axis=3, tiled=True)  23.4 us
    all_to_all x1, waiting for transfers between devices, local(): lax.all_to_all(lax.all_to_all(outgoing, ('row', 'col'), split_axis=0, con...  13.6 us
    all_to_all x1, starting transfers between devices, local(): lax.all_to_all(lax.all_to_all(outgoing, ('row', 'col'), split_axis=0, con...  8.58 us
    all_gather x1, local copies, waits for them, and re-layouts, local(): full_d = lax.all_gather(integrals, 'col', axis=3, tiled=True)  7.66 us
    dot_general x1, matrix products, contract(): lax.dot_general(amp_rows, block, (((1, 2), (2, 3)), ((), ())), preferred_...  6.25 us
  transfers between devices with their start and end apart: 2, of which 2 were waited for; matrix products, arithmetic and copies ran while one was open for 2% of the time, Pallas kernels for 0%

commit v1 on v0

v1 whole, which is shorter than its diff:
```python
import jax
import jax.numpy as jnp
from jax import lax
from jax.experimental import pallas as pl
from jax.experimental.pallas import tpu as pltpu
from jax.sharding import PartitionSpec as P

NO = 128
NV = 1792
SA = 64
CW = 3
VBLK = 16
KK = CW * NV
NX, NY, NZL = 4, 8, 4
DW = NV // NY
PIECE = CW * 256
MESH = pl.DeviceIdType.MESH
NT = (((1,), (1,)), ((), ()))
NN = (((1,), (0,)), ((), ()))


def dev(x, y, z, k):
    return (lax.rem(z, NZL) * NX + x, y, lax.div(z, NZL) * 2 + k)


def dot(a, b, dims=NN):
    return lax.dot_general(a, b, dims, preferred_element_type=jnp.float32)


def iota2(shape):
    return (
        lax.broadcasted_iota(jnp.int32, shape, 0),
        lax.broadcasted_iota(jnp.int32, shape, 1),
    )


def ones_where(cond):
    return jnp.where(cond, 1.0, 0.0).astype(jnp.bfloat16)


def kernel(
    t_ref, v_ref, a_ref, w_ref, ps_ref, ea_ref, eb_ref, out_ref,
    t_all, v_stage, v_all, a_all, acc, lhs_hi, lhs_lo, place, mail, d_all, rec, swap, sbuf, order,
    t_own_sem, ty_send, ty_recv, tf_send, tf_recv, sib_send, sib_recv,
    vy_send, vy_recv, vx_send, vx_recv, vf_send, vf_recv,
    a_send, a_recv, d_send, d_recv, m_send, m_recv,
):
    r = lax.axis_index("row")
    y = lax.axis_index("col")
    v = lax.axis_index("vir")
    x, zl = lax.rem(r, NX), lax.div(r, NX)
    zh, k = lax.div(v, 2), lax.rem(v, 2)
    z = zh * NZL + zl
    xs = (lax.rem(x + 1, NX), lax.rem(x + NX - 1, NX))
    ys = (lax.rem(y + 1, NY), lax.rem(y + NY - 1, NY))
    zs = (lax.rem(z + 1, 8), lax.rem(z + 7, 8))
    is_self = zl == v

    own = pltpu.make_async_copy(t_ref, t_all.at[pl.ds(0, 128)], t_own_sem)
    own.start()

    barrier = pltpu.get_barrier_semaphore()

    def greet(where):
        pl.semaphore_signal(barrier, inc=1, device_id=where, device_id_type=MESH)

    for d in range(2):
        greet(dev(x, ys[d], z, k))
        greet(dev(xs[d], y, z, k))
        greet(dev(x, y, zs[d], k))
    greet(dev(x, y, z, 1 - k))

    def greet_slab(n, carry):
        nz, ny = lax.div(n, NY), lax.rem(n, NY)
        greet(dev(x, lax.rem(y + ny, NY), zh * NZL + lax.rem(zl + nz, NZL), k))
        return carry

    lax.fori_loop(1, 32, greet_slab, 0)

    def greet_mail(n, carry):
        sx, sy, sv = lax.rem(n, 4), lax.rem(lax.div(n, 4), 8), lax.div(n, 32)
        row = v * NX + sx
        mine = jnp.logical_and(jnp.logical_and(row == r, sy == y), sv == v)

        @pl.when(jnp.logical_not(mine))
        def _():
            greet((row, sy, sv))

        return carry

    lax.fori_loop(0, 128, greet_mail, 0)
    pl.semaphore_wait(barrier, 7 + 31 + 128 - jnp.where(is_self, 1, 0))
    own.wait()

    def remote(src, dst, send, recv, where):
        return pltpu.make_async_remote_copy(
            src_ref=src, dst_ref=dst, send_sem=send, recv_sem=recv, device_id=where, device_id_type=MESH
        )

    sends = []

    def go(copy):
        copy.start()
        sends.append(copy)

    def t_rows(block, h):
        return pl.ds(pl.multiple_of(block * 128 + k * 64 + h * 32, 32), 32)

    t_block = (3, 1)

    def t_copy(d, h):
        return remote(
            t_all.at[t_rows(0, h)], t_all.at[t_rows(t_block[d], h)], ty_send.at[d, h], ty_recv.at[d, h],
            dev(x, y, zs[d], k),
        )

    def t_forward(d):
        h = d
        return remote(
            t_all.at[t_rows(t_block[d], h)], t_all.at[t_rows(2, h)], tf_send.at[d], tf_recv.at[d],
            dev(x, y, zs[d], k),
        )

    def t_sibling(block, h):
        rows = t_rows(block, h)
        return remote(
            t_all.at[rows], t_all.at[rows], sib_send.at[block - 1, h], sib_recv.at[block - 1, h],
            dev(x, y, z, 1 - k),
        )

    def vy_copy(d, s, h):
        slot = lax.rem(y + (NY - s if d == 0 else s), NY)
        rows = pl.ds(h * 32, 32)
        return remote(
            v_stage.at[slot, rows], v_stage.at[slot, rows], vy_send.at[d, s, h], vy_recv.at[d, s, h],
            dev(x, ys[d], z, k),
        )

    def v_rows(slot, h):
        return pl.ds(pl.multiple_of(slot * 64 + h * 32, 32), 32)

    def vx_copy(d, h):
        rows = v_rows(x, h)
        return remote(
            v_all.at[rows], v_all.at[rows], vx_send.at[d, h], vx_recv.at[d, h], dev(xs[d], y, z, k)
        )

    def vx_forward(d):
        rows = v_rows(xs[1 - d], d)
        return remote(
            v_all.at[rows], v_all.at[rows], vf_send.at[d], vf_recv.at[d], dev(xs[d], y, z, k)
        )

    v_stage[y] = v_ref[...]
    a_all[y] = a_ref[...]
    for h in range(2):
        go(vy_copy(0, 0, h))
        go(vy_copy(1, 0, h))
    go(t_copy(0, 0))
    go(t_copy(1, 1))
    go(t_copy(0, 1))
    go(t_copy(1, 0))

    def slab_copy(n):
        nz, ny = lax.div(n, NY), lax.rem(n, NY)
        block = lax.rem(NZL - nz, NZL)
        return remote(
            a_ref, a_all.at[block * NY + y], a_send, a_recv,
            dev(x, lax.rem(y + ny, NY), zh * NZL + lax.rem(zl + nz, NZL), k),
        )

    def send_slab(n, carry):
        slab_copy(n).start()
        return carry

    lax.fori_loop(1, 32, send_slab, 0)

    for s in range(4):
        for h in range(2):
            vy_copy(0, s, h).wait_recv()
            if s < 3:
                go(vy_copy(0, s + 1, h))
                vy_copy(1, s, h).wait_recv()
            if s < 2:
                go(vy_copy(1, s + 1, h))
            if s == 3:
                rows = pl.ds(h * 32, 32)
                for c in range(CW):
                    for half in range(2):
                        joined = jnp.concatenate(
                            [v_stage[half * 4 + q, rows, c * 256 : c * 256 + DW] for q in range(4)], axis=1
                        )
                        v_all[v_rows(x, h), c * NV + half * 896 : c * NV + (half + 1) * 896] = joined
                go(vx_copy(0, h))
                go(vx_copy(1, h))

    m, n = iota2((2048, 256))
    place[...] = ones_where(jnp.logical_and(m >> 7 == n >> 4, (m & 15) == (n & 15)))
    m, n = iota2((256, 256))
    swap[...] = ones_where(jnp.logical_and(m >> 4 == (n & 15), (m & 15) == n >> 4))

    def build_order(i, carry):
        m, n = iota2((256, 1024))
        hit = jnp.logical_and(m >> 4 == n >> 6, (m & 15) == (n & 15))
        hit = jnp.logical_and(hit, ((n >> 4) & 3) == i)
        order[pl.ds(pl.multiple_of(i * 256, 256), 256), :] = ones_where(hit)
        return carry

    lax.fori_loop(0, 4, build_order, 0)

    t_copy(0, 0).wait_recv()
    go(t_forward(0))
    go(t_sibling(3, 0))
    t_copy(1, 1).wait_recv()
    go(t_forward(1))
    go(t_sibling(1, 1))

    pltpu.make_async_copy(a_all.at[pl.ds(0, 31)], a_all.at[pl.ds(0, 31)], a_recv).wait()
    m, n = iota2((32, 128))
    keep = m >> 2 == n >> 4

    def crossed(block, carry):
        slab = a_all[pl.ds(block * NY, NY)].reshape(NO * CW, 128)
        zr = dot(w_ref[...], slab)
        for b in range(16):
            for q in range(4):
                part = zr[b * 32 + q * 8 : b * 32 + q * 8 + 8, :]
                wide = jnp.where(keep, jnp.concatenate([part] * 4, axis=0), 0.0)
                hi = wide.astype(jnp.bfloat16)
                lhs_hi[q * 32 : q * 32 + 32, b * 128 : b * 128 + 128] = hi
                lhs_lo[q * 32 : q * 32 + 32, b * 128 : b * 128 + 128] = (
                    wide - hi.astype(jnp.float32)
                ).astype(jnp.bfloat16)
        rows = pl.ds(pl.multiple_of(block * 128, 128), 128)
        acc[rows, :] = dot(lhs_hi[...], place[...]) + dot(lhs_lo[...], place[...])
        return carry

    lax.fori_loop(0, 4, crossed, 0)

    vx_copy(0, 0).wait_recv()
    go(vx_forward(0))
    t_copy(0, 1).wait_recv()
    go(t_sibling(3, 1))
    t_copy(1, 0).wait_recv()
    go(t_sibling(1, 0))
    vx_copy(1, 1).wait_recv()
    go(vx_forward(1))
    vx_copy(0, 1).wait_recv()
    vx_copy(1, 0).wait_recv()
    for d in range(2):
        t_forward(d).wait_recv()
        go(t_sibling(2, d))
    for d in range(2):
        vx_forward(d).wait_recv()
    for block in (3, 1, 2):
        for h in range(2):
            t_sibling(block, h).wait_recv()

    def ladder(i, carry):
        ks = pl.ds(pl.multiple_of(i * 768, 768), 768)
        acc[...] += dot(t_all[:, ks], v_all[:, ks], NT)
        return carry

    lax.fori_loop(0, KK // 768, ladder, 0)

    for block in range(1, 4):
        there = zh * NZL + lax.rem(zl + block, NZL)
        copy = remote(
            acc.at[pl.ds(block * 128, 128)], d_all.at[zl], d_send.at[block - 1], d_recv, dev(x, y, there, k)
        )
        go(copy)
    d_all[zl] = acc[pl.ds(0, 128), :]

    for block in range(4):
        for h in range(2):
            mail[:, block * 2 + h, :] = acc[block * 128 : block * 128 + 128, h * 128 : h * 128 + 128]
    here = v * 32 + y * 4 + x

    def send_mail(n, carry):
        pj = lax.rem(r + n, 16)
        qi = lax.rem(y + lax.div(n, 16), NY)
        tile = lax.div(pj, 4) * 32 + qi * 4 + lax.rem(pj, 4)
        mine = jnp.logical_and(is_self, n == 0)

        @pl.when(mine)
        def _():
            pltpu.make_async_copy(mail.at[tile], rec.at[here], m_recv).start()

        @pl.when(jnp.logical_not(mine))
        def _():
            remote(mail.at[tile], rec.at[here], m_send, m_recv, (pj, qi, zl)).start()

        return carry

    lax.fori_loop(0, 128, send_mail, 0)

    pltpu.make_async_copy(d_all.at[pl.ds(0, 3)], d_all.at[pl.ds(0, 3)], d_recv).wait()
    pltpu.make_async_copy(rec, rec, m_recv).wait()

    for vb in range(4):
        part = d_all[vb]
        hi = part.astype(jnp.bfloat16)
        rest = part - hi.astype(jnp.float32)
        mid = rest.astype(jnp.bfloat16)
        low = (rest - mid.astype(jnp.float32)).astype(jnp.bfloat16)
        d_all[vb] = dot(hi, swap[...]) + (dot(mid, swap[...]) + dot(low, swap[...]))
    for block in range(4):
        zj = lax.rem(v + block, 4)
        rows = pl.ds(pl.multiple_of(zj * 32, 32), 32)
        pair = ps_ref[rows, :]
        for vb in range(4):
            mirrored = jnp.concatenate(
                [rec[vb * 32 : vb * 32 + 32, block * 2 + h, :] for h in range(2)], axis=1
            )
            denom = (pair - ea_ref[...]) - eb_ref[vb : vb + 1, :]
            res = (d_all[vb, rows, :] + mirrored) / denom
            sbuf[rows, vb * 256 : vb * 256 + 256] = res.astype(jnp.bfloat16)
    out_ref[...] = dot(sbuf[...], order[...]).astype(jnp.bfloat16)

    for copy in sends:
        copy.wait_send()
    pltpu.make_async_copy(a_all.at[pl.ds(0, 31)], a_all.at[pl.ds(0, 31)], a_send).wait()

    @pl.when(is_self)
    def _():
        pltpu.make_async_copy(mail.at[pl.ds(0, 127)], mail.at[pl.ds(0, 127)], m_send).wait()

    @pl.when(jnp.logical_not(is_self))
    def _():
        pltpu.make_async_copy(mail, mail, m_send).wait()


def call(t, vv, a, w, ps, ea, eb):
    bf, f32 = jnp.bfloat16, jnp.float32
    vm = pl.BlockSpec(memory_space=pltpu.VMEM)
    dma = pltpu.SemaphoreType.DMA
    return pl.pallas_call(
        kernel,
        out_shape=jax.ShapeDtypeStruct((NO, 1024), bf),
        in_specs=[pl.BlockSpec(memory_space=pl.ANY)] + [vm] * 6,
        out_specs=vm,
        scratch_shapes=[
            pltpu.VMEM((512, KK), bf),
            pltpu.VMEM((NY, 64, PIECE), bf),
            pltpu.VMEM((256, KK), bf),
            pltpu.VMEM((32, 48, 128), bf),
            pltpu.VMEM((512, 256), f32),
            pltpu.VMEM((128, 2048), bf),
            pltpu.VMEM((128, 2048), bf),
            pltpu.VMEM((2048, 256), bf),
            pltpu.VMEM((128, 8, 128), f32),
            pltpu.VMEM((4, 128, 256), f32),
            pltpu.VMEM((128, 8, 128), f32),
            pltpu.VMEM((256, 256), bf),
            pltpu.VMEM((128, 1024), bf),
            pltpu.VMEM((1024, 1024), bf),
            dma,
            dma((2, 2)), dma((2, 2)), dma((2,)), dma((2,)), dma((3, 2)), dma((3, 2)),
            dma((2, 4, 2)), dma((2, 4, 2)), dma((2, 2)), dma((2, 2)), dma((2,)), dma((2,)),
            dma, dma, dma((3,)), dma, dma, dma,
        ],
        compiler_params=pltpu.CompilerParams(
            collective_id=0, has_side_effects=True, vmem_limit_bytes=48 * 1024 * 1024
        ),
        cost_estimate=pl.CostEstimate(flops=2 * 512 * 256 * KK, bytes_accessed=20_000_000, transcendentals=0),
    )(t, vv, a, w, ps, ea, eb)


def local(amplitudes, integrals, hole_integrals, irreps, occ_energy, vir_energy):
    r = lax.axis_index("row")
    y = lax.axis_index("col")
    v = lax.axis_index("vir")
    zl = lax.div(r, NX)
    amps = amplitudes.reshape(8, 4, 4, CW, NV)
    t = jnp.transpose(amps, (1, 0, 2, 3, 4)).reshape(NO, KK)
    labels = jnp.repeat(irreps, VBLK)
    lab_a = lax.dynamic_slice_in_dim(labels, v * 16, 16)
    lab_b = lax.dynamic_slice_in_dim(labels, r * 4, 4)
    lab_d = lax.dynamic_slice_in_dim(labels, y * DW, DW)
    left = jnp.bitwise_xor(lab_a[:, None], lab_b[None, :])
    right = jnp.bitwise_xor(labels[:CW][:, None], lab_d[None, :])
    keep = left[:, :, None, None] == right[None, None, :, :]
    masked = jnp.where(keep, integrals, jnp.zeros_like(integrals))
    masked = jnp.transpose(masked, (1, 0, 2, 3)).reshape(64, CW, DW)
    vv = jnp.pad(masked, ((0, 0), (0, 0), (0, 256 - DW))).reshape(64, PIECE)
    slab = lax.dynamic_slice_in_dim(amplitudes, v * 16, 16, 6).reshape(8, 16, CW, 16)
    a = jnp.transpose(slab, (1, 2, 0, 3)).reshape(48, 128)
    hole = lax.dynamic_slice_in_dim(hole_integrals, zl * 16, 16, 5).reshape(NO, 4, 1, 4, CW, 16)
    hole = jnp.broadcast_to(hole, (NO, 4, 2, 4, CW, 16))
    w = -jnp.transpose(hole, (5, 1, 2, 3, 0, 4)).reshape(512, NO * CW)
    energy_i = lax.dynamic_slice_in_dim(occ_energy.reshape(8, 16), r, 1, 1).reshape(1, 8, 1)
    energy_j = lax.dynamic_slice_in_dim(occ_energy.reshape(8, 16), y, 1, 0).reshape(4, 1, 4)
    ps = (energy_i + energy_j).reshape(NO, 1)
    energy_a = lax.dynamic_slice_in_dim(vir_energy, v * 16, 16)
    ea = jnp.broadcast_to(energy_a[:, None], (16, 16)).reshape(1, 256)
    eb = jnp.broadcast_to(vir_energy.reshape(4, 1, 16), (4, 16, 16)).reshape(4, 256)
    out = call(t, vv, a, w, ps, ea, eb)
    out = jnp.transpose(out.reshape(4, 8, 4, 16, SA), (1, 0, 2, 3, 4))
    return out.reshape(8, 1, 1, 1, 16, 16, SA)


def solution(mesh):
    in_specs = (
        P(None, "row", None, "col", None, None, None),
        P("vir", "row", None, "col"),
        P(None, None, "col", None, None, None),
        P(),
        P(),
        P(),
    )
    out_specs = P(None, "row", None, "col", None, "vir", None)
    return jax.shard_map(local, mesh=mesh, in_specs=in_specs, out_specs=out_specs, check_vma=False)
```

time: 290 us -> 146 us (0.50)
  waiting for transfers between devices: 125 us -> 0 us
  blocking collectives: 107 us -> 0 us
  Pallas kernels: 0 us -> 90.4 us
  local copies, waits for them, and re-layouts: 26.1 us -> 53.2 us
  between operations: 13.6 us -> 0.17 us
  starting transfers between devices: 8.58 us -> 0 us
  matrix products: 6.9 us -> 0 us
    all_gather x1 -> x0, waiting for transfers between devices: 111 us -> none  [local(): piece = lax.all_gather(full_d, 'row', axis=1, tiled=True)]
    pallas_call x0 -> x1, Pallas kernels: none -> 90.4 us  [call(): pl.pallas_call(kernel, out_shape=jax.ShapeDtypeStruct((NO, 1024), bf), in...]
    all_gather x2 -> x0, blocking collectives: 78.2 us -> none  [the longest x1 54.8 us: local(): full_d = lax.all_gather(integrals, 'col', axis=3, tiled=True)]
    neg x0 -> x4, local copies, waits for them, and re-layouts: none -> 48.9 us  [local(): w = -jnp.transpose(hole, (5, 1, 2, 3, 0, 4)).reshape(512, NO * CW)]
    all_to_all x1 -> x0, blocking collectives: 28.9 us -> none  [local(): lax.all_to_all(outgoing, ('row', 'col'), split_axis=0, concat_axis=0, til...]
    all_to_all x1 -> x0, waiting for transfers between devices: 13.6 us -> none  [local(): lax.all_to_all(lax.all_to_all(outgoing, ('row', 'col'), split_axis=0, con...]
    all_to_all x1 -> x0, starting transfers between devices: 8.58 us -> none  [local(): lax.all_to_all(lax.all_to_all(outgoing, ('row', 'col'), split_axis=0, con...]
    all_gather x2 -> x0, local copies, waits for them, and re-layouts: 8.13 us -> none  [the longest x1 7.66 us: local(): full_d = lax.all_gather(integrals, 'col', axis=3, tiled=True)]
  transfers between devices with their start and end apart: 2 -> 0, of which waited for: 2 -> 0; matrix products, arithmetic and copies ran while one was open for 2% -> 0% of each run, Pallas kernels for 0% -> 0%
where the time goes in v1:
time: 146 us; the launch traced here: 145 us
  Pallas kernels  90.4 us (62%)
  local copies, waits for them, and re-layouts  53.2 us (36%)
    pallas_call x1, Pallas kernels, call(): pl.pallas_call(kernel, out_shape=jax.ShapeDtypeStruct((NO, 1024), bf), in...  90.4 us
    neg x4, local copies, waits for them, and re-layouts, local(): w = -jnp.transpose(hole, (5, 1, 2, 3, 0, 4)).reshape(512, NO * CW)  48.9 us

profile of v1, /device:TPU:1, one launch (start us, length us, event | category | flops | bytes accessed | tf_op | source)
XLA Modules:
  0.0 145.0 jit_solution(16448392003960382463)
XLA Ops:
  0.0 1.0 dynamic-slice_negate_fusion
  1.0 10.8 %copy.15 = bf16[128,4,4,3,16]{2,1,4,3,0:T(4,128)(2,1)} copy(bf16[128,4,4,3,16]{0,4,3,2,1:T(8,128)(2,1)S(1)} %bitcast.30) | data formatting | bytes 393216 | tf_op jit(solution)/shard_map/neg | solution.py:390
  11.8 13.1 %broadcast_bitcast_fusion = bf16[16,4,2,4,128,3]{3,2,1,0,5,4:T(2,128)(2,1)} fusion(bf16[128,4,4,3,16]{2,1,4,3,0:T(4,128)(2,1)} %copy.15), kind=kLoop, calls=%fused_computation | loop fusion | bytes 589824 | tf_op jit(solution)/shard_map/neg | solution.py:390
  24.9 0.0 copy-start.2
  24.9 0.0 copy-start.1
  24.9 24.8 %neg.12 = bf16[512,384]{0,1:T(8,128)(2,1)S(1)} reshape(bf16[16,4,2,4,128,3]{3,2,1,0,5,4:T(2,128)(2,1)} %broadcast_bitcast_fusion) | data formatting | bytes 786432 | tf_op jit(solution)/shard_map/neg | solution.py:390
  49.7 0.0 copy-start.3
  49.7 0.0 copy-start
  49.7 0.0 copy-start.4
  49.7 0.2 copy.16.w_ref
  49.9 0.0 copy-done.2
  50.0 0.1 broadcast_in_dim.12
  50.0 0.1 reshape.128
  50.1 0.1 dynamic_slice.25
  50.2 0.1 dynamic_slice.24
  50.3 0.1 broadcast_xor_fusion.1
  50.3 0.1 dynamic_slice.26
  50.4 0.1 broadcast_xor_fusion
  50.5 0.0 copy-done.1
  50.5 0.1 compare_select_fusion
  50.6 0.1 copy.19
  50.7 0.1 pad.4.clone
  50.8 0.0 copy-done.3
  50.8 0.1 reshape.133
  50.9 0.2 dynamic-slice_reduce_fusion
  51.1 0.1 add.59
  51.2 0.1 broadcast_add_fusion
  51.2 0.1 add.64.ps_ref
  51.3 0.0 copy-done
  51.3 0.1 dynamic-slice_bitcast_fusion
  51.5 0.1 reshape.132.a_ref
  51.6 0.0 copy-done.4
  51.6 0.1 dynamic_slice.31
  51.7 0.1 broadcast_in_dim.15
  51.8 0.1 reshape.134.ea_ref
  51.8 0.3 reshape.126
  52.2 0.9 copy.11
  53.1 0.1 copy.20
  53.3 0.1 broadcast_in_dim.16
  53.4 0.1 reshape.135.eb_ref
  53.5 90.4 %shard_map.64 = bf16[128,1024]{1,0:T(8,128)(2,1)S(1)} custom-call(bf16[128,5376]{1,0:T(8,128)(2,1)S(1)} %bitcast.26, bf16[64,768]{1,0:T(8,128)(2,1)S(1)} %bitcast.27, bf16[48,128]{1,0:T(8,128)(2,1)S(1)} %reshape.132.a_ref, bf16[512,384]{1,0:T(8,128)(2,1)S(1)} %copy.16.w_ref, f32[128,1]{1,0:T(8,128)S(1)} %add.64.ps_ref, f32[1,256]{1,0:T(1,128)S(1)} %reshape.134.ea_ref, ...), custom_call_target="tpu_custom_call" | custom-call | flops 1409286144 | bytes 20000000 | tf_op jit(solution)/shard_map/pallas_call | solution.py:337
  143.8 0.3 reshape.136
  144.2 0.8 copy.18
  (5 shorter events, 0.1 us)
Async XLA Ops:
  24.9 25.1 %copy-start.2 = (s32[112]{0:T(128)S(1)}, s32[112]{0:T(128)}, u32[]{:S(2)}) copy-start(s32[112]{0:T(128)} %param.9) | copy-start | bytes 1348
  24.9 25.6 %copy-start.1 = (bf16[16,4,3,224]{3,1,2,0:T(4,128)(2,1)S(1)}, bf16[16,4,3,224]{3,1,2,0:T(4,128)(2,1)}, u32[]{:S(2)}) copy-start(bf16[16,4,3,224]{3,1,2,0:T(4,128)(2,1)} %param.7) | copy-start | bytes 258052
  49.7 1.1 copy-start.3
  49.7 1.6 %copy-start = (bf16[8,1,1,1,16,3,1792]{6,4,5,3,2,1,0:T(8,128)(2,1)S(1)}, bf16[8,1,1,1,16,3,1792]{6,4,5,3,2,1,0:T(8,128)(2,1)}, u32[]{:S(2)}) copy-start(bf16[8,1,1,1,16,3,1792]{6,4,5,3,2,1,0:T(8,128)(2,1)} %param.6) | copy-start | bytes 4128772
  49.7 1.9 %copy-start.4 = (f32[64]{0:T(128)S(1)}, f32[64]{0:T(128)}, u32[]{:S(2)}) copy-start(f32[64]{0:T(128)} %param.11) | copy-start | bytes 772

commit v2 on v0

v2 whole, which is shorter than its diff:
```python
import jax
import jax.numpy as jnp
from jax import lax
from jax.experimental import pallas as pl
from jax.experimental.pallas import tpu as pltpu
from jax.sharding import PartitionSpec as P

NO = 128
NV = 1792
SA = 64
CW = 3
VBLK = 16
KK = CW * NV
NX, NY, NZ, NZL = 4, 8, 8, 4
DW = NV // NY
PIECE = CW * 256
MESH = pl.DeviceIdType.MESH
NT = (((1,), (1,)), ((), ()))
NN = (((1,), (0,)), ((), ()))

WORK = [
    (0, 1), (1, 0), (0, 0), (1, 1), (2, 1), (1, 2), (0, 3), (3, 0),
    (2, 0), (0, 2), (1, 3), (3, 1), (2, 2), (3, 3), (2, 3), (3, 2),
]
PLACE_OF = [WORK.index((a, b)) for a in range(4) for b in range(4)]


def pick(index, table):
    value = jnp.int32(table[0])
    for n in range(1, len(table)):
        value = jnp.where(index == n, jnp.int32(table[n]), value)
    return value


def dev(x, y, z, k):
    return (lax.rem(z, NZL) * NX + x, y, lax.div(z, NZL) * 2 + k)


def dot(a, b, dims=NN):
    return lax.dot_general(a, b, dims, preferred_element_type=jnp.float32)


def remote(src, dst, send, recv, where):
    return pltpu.make_async_remote_copy(
        src_ref=src, dst_ref=dst, send_sem=send, recv_sem=recv, device_id=where, device_id_type=MESH
    )


def kernel(
    t_ref, v_ref, w_ref, irreps, occ, vir, out_ref,
    t_all, s0, s1, v_all, a_mat, zs, acc, own_x, order, swap, pull, a_own, v_own, w_own, denom, mail, rec, sbuf, d_all,
    ssem, rsem, load_sem, a_send, a_recv, m_send, m_recv, d_recv,
):
    r = lax.axis_index("row")
    y = lax.axis_index("col")
    v = lax.axis_index("vir")
    x, zl = lax.rem(r, NX), lax.div(r, NX)
    zh, k = lax.div(v, 2), lax.rem(v, 2)
    z = zh * NZL + zl
    xs = (lax.rem(x + 1, NX), lax.rem(x + NX - 1, NX))
    ys = (lax.rem(y + 1, NY), lax.rem(y + NY - 1, NY))
    zn = (lax.rem(z + 1, NZ), lax.rem(z + NZ - 1, NZ))
    blk_a = pick(z * 2 + k, [w[0] for w in WORK])
    blk_b = pick(z * 2 + k, [w[1] for w in WORK])
    diag = blk_a == blk_b
    own = blk_a == v
    twin = jnp.where(diag, k, 1 - k)

    t_loads = [
        pltpu.make_async_copy(
            t_ref.at[:, c], t_all.at[pl.ds(0, 8), :, pl.ds(c * NV, NV)], load_sem.at[c]
        )
        for c in range(CW)
    ]
    w_load = pltpu.make_async_copy(w_ref, w_own, load_sem.at[3])
    for load in t_loads:
        load.start()
    w_load.start()

    barrier = pltpu.get_barrier_semaphore()

    def greet(where):
        pl.semaphore_signal(barrier, inc=1, device_id=where, device_id_type=MESH)

    for n in range(1, NX):
        greet(dev(lax.rem(x + n, NX), y, z, k))

    def greet_y(n, carry):
        greet(dev(x, lax.rem(y + n, NY), z, k))
        return carry

    lax.fori_loop(1, NY, greet_y, 0)

    def greet_z(n, carry):
        other = lax.rem(z * 2 + k + n, 16)
        greet(dev(x, y, lax.div(other, 2), lax.rem(other, 2)))
        return carry

    lax.fori_loop(1, 16, greet_z, 0)
    first = jnp.where(diag, 1, 0)

    def partner(n):
        return (lax.rem(x + lax.rem(n, NX), NX), lax.rem(y + lax.div(n, NX), NY))

    def greet_mail(n, carry):
        px, py = partner(n)
        greet(dev(px, py, z, twin))
        return carry

    lax.fori_loop(first, 32, greet_mail, 0)
    label = jnp.bitwise_xor(jnp.bitwise_xor(irreps[v], irreps[zl]), irreps[0])
    lane = lax.broadcasted_iota(jnp.int32, (8, PIECE), 1) & 255
    kept = jnp.zeros((8, PIECE), jnp.float32)
    for n in range(DW // VBLK):
        same = jnp.where(irreps[y * (DW // VBLK) + n] == label, 1.0, 0.0)
        kept = jnp.where(lane >> 4 == n, same, kept)
    v_own[...] = (v_ref[...].astype(jnp.float32) * kept[0:1]).astype(jnp.bfloat16)

    m = lax.broadcasted_iota(jnp.int32, (1024, 128), 0)
    n = lax.broadcasted_iota(jnp.int32, (1024, 128), 1)
    hit = jnp.logical_and(m >> 7 == n >> 4, (m & 127) == (n & 15) + v * 16)
    pull[...] = jnp.where(hit, 1.0, 0.0).astype(jnp.bfloat16)
    for load in t_loads:
        load.wait()
    for c in range(CW):
        wide = jnp.concatenate([t_all[q, :, c * NV : c * NV + 128] for q in range(8)], axis=1)
        a_own[c] = dot(wide, pull[...]).astype(jnp.bfloat16)
    pl.semaphore_wait(barrier, 3 + 7 + 15 + 32 - first)

    names = {}
    sends = []

    def sem(*name):
        return names.setdefault(name, len(names))

    def hop(src, dst, where, *name):
        n = sem(*name)
        return remote(src, dst, ssem.at[n], rsem.at[n], where)

    def go(copy):
        copy.start()
        sends.append(copy)

    t_block = (3, 1)

    def t_rows(block, h):
        return t_all.at[pl.ds(block * 8 + k * 4 + h * 2, 2)]

    def t_copy(d, h):
        return hop(t_rows(0, h), t_rows(t_block[d], h), dev(x, y, zn[d], k), "t", d, h)

    def t_forward(d):
        return hop(t_rows(t_block[d], d), t_rows(2, d), dev(x, y, zn[d], k), "tf", d)

    def t_sibling(block, h):
        return hop(t_rows(block, h), t_rows(block, h), dev(x, y, z, 1 - k), "ts", block, h)

    def slab_place(block):
        rows = pl.ds(pl.multiple_of(y * 16, 16), 16)
        return a_mat.at[:, rows, pl.ds(pl.multiple_of(block * 128, 128), 128)]

    slab_rows = a_mat.at[:, pl.ds(pl.multiple_of(y * 16, 16), 16), :]

    def slab_y(d, s):
        slot = lax.rem(y + (NY - s if d == 0 else s), NY)
        part = a_mat.at[:, pl.ds(pl.multiple_of(slot * 16, 16), 16), :]
        return hop(part, part, dev(x, ys[d], z, k), "b", d, s)

    def v0_y(d, s):
        slot = s0.at[lax.rem(y + (NY - s if d == 0 else s), NY)]
        return hop(slot, slot, dev(x, ys[d], z, k), "v0y", d, s)

    def v0_rows(slot, part):
        return v_all.at[pl.ds(pl.multiple_of(slot * 64 + part * 16, 16), 16)]

    def v0_x(d, part):
        rows = v0_rows(x, part)
        return hop(rows, rows, dev(xs[d], y, z, k), "v0x", d, part)

    def v0_f(d):
        rows = v0_rows(xs[1 - d], d)
        return hop(rows, rows, dev(xs[d], y, z, k), "v0f", d)

    def v1_x(n):
        slot = s1.at[y, x]
        return hop(slot, slot, dev(lax.rem(x + n, NX), y, z, k), "v1x", n)

    def v1_y(d, s, e):
        slot = s1.at[lax.rem(y + (NY - s if d == 0 else s), NY), pl.ds(2 * e, 2)]
        return hop(slot, slot, dev(x, ys[d], z, k), "v1y", d, s, e)

    there = pick(v * 4 + zl, PLACE_OF)
    moves = there != z * 2 + k
    go_there = dev(x, y, lax.div(there, 2), lax.rem(there, 2))
    raw = [
        (v_own.at[pl.ds(0, 32)], s0.at[y], sem("r", 0)),
        (v_own.at[pl.ds(32, 32)], s1.at[y, x], sem("r", 1)),
    ]

    @pl.when(moves)
    def _():
        for src, dst, n in raw:
            remote(src, dst, ssem.at[n], rsem.at[n], go_there).start()

    @pl.when(jnp.logical_not(moves))
    def _():
        for src, dst, n in raw:
            pltpu.make_async_copy(src, dst, rsem.at[n]).start()

    for b in range(4):
        at = pick(v * 4 + b, PLACE_OF)
        az, ak = lax.div(at, 2), lax.rem(at, 2)
        block = lax.rem(zl - lax.rem(az, NZL) + NZL, NZL)
        mine = at == z * 2 + k

        @pl.when(mine)
        def _():
            pltpu.make_async_copy(a_own, slab_place(0), a_recv).start()

        @pl.when(jnp.logical_not(mine))
        def _():
            remote(a_own, slab_place(block), a_send, a_recv, dev(x, y, az, ak)).start()

    go(t_copy(0, 0))
    go(t_copy(1, 1))
    go(t_copy(0, 1))
    go(t_copy(1, 0))
    for src, dst, n in raw:
        pltpu.make_async_copy(src, dst, rsem.at[n]).wait()
        if n == raw[0][2]:
            go(v0_y(0, 0))
            go(v0_y(1, 0))
    for n in range(1, NX):
        go(v1_x(n))

    def v0_step(s):
        v0_y(0, s).wait_recv()
        if s < 3:
            go(v0_y(0, s + 1))
            v0_y(1, s).wait_recv()
        if s < 2:
            go(v0_y(1, s + 1))

    def v1_step(s):
        for e in range(2):
            for d in range(2):
                if s == 3 and d != e:
                    continue
                v1_y(d, s, e).wait_recv()
                if s < 2 or (s == 2 and d == e):
                    go(v1_y(d, s + 1, e))

    def slab_step(s):
        for d in range(2):
            if s == 3 and d == 1:
                continue
            slab_y(d, s).wait_recv()
            if s < 3 - d:
                go(slab_y(d, s + 1))

    def join(source, rows):
        for c in range(CW):
            for half in range(2):
                joined = jnp.concatenate(
                    [source[half * 4 + q][:, c * 256 : c * 256 + DW] for q in range(4)], axis=1
                )
                v_all[rows, c * NV + half * 896 : c * NV + (half + 1) * 896] = joined

    v0_step(0)
    for n in range(1, NX):
        v1_x(n).wait_recv()
    for e in range(2):
        go(v1_y(0, 0, e))
        go(v1_y(1, 0, e))
    v0_step(1)
    pltpu.make_async_copy(slab_rows, slab_rows, a_recv).wait()
    go(slab_y(0, 0))
    go(slab_y(1, 0))
    v0_step(2)
    t_copy(0, 0).wait_recv()
    go(t_forward(0))
    go(t_sibling(3, 0))
    t_copy(1, 1).wait_recv()
    go(t_forward(1))
    go(t_sibling(1, 1))
    v1_step(0)
    slab_step(0)
    v0_step(3)
    join([s0.at[q] for q in range(NY)], pl.ds(pl.multiple_of(x * 64, 32), 32))
    go(v0_x(0, 0))
    go(v0_x(1, 1))
    go(v0_x(0, 1))
    go(v0_x(1, 0))
    slab_step(1)
    m = lax.broadcasted_iota(jnp.int32, (256, 256), 0)
    n = lax.broadcasted_iota(jnp.int32, (256, 256), 1)
    hit = jnp.logical_and(m >> 4 == (n & 15), (m & 15) == n >> 4)
    swap[...] = jnp.where(hit, 1.0, 0.0).astype(jnp.bfloat16)
    lane = lax.broadcasted_iota(jnp.int32, (16, 256), 1)
    line = lax.broadcasted_iota(jnp.int32, (16, 256), 0)
    e_j = jnp.zeros((16, 256), jnp.float32)
    e_a = jnp.zeros((16, 256), jnp.float32)
    e_b = jnp.zeros((16, 256), jnp.float32)
    for n in range(16):
        e_j = jnp.where(line == n, occ[y * 16 + n], e_j)
        e_a = jnp.where(lane >> 4 == n, vir[blk_a * 16 + n], e_a)
        e_b = jnp.where((lane & 15) == n, vir[blk_b * 16 + n], e_b)
    for block in range(4):
        for q in range(8):
            e_i = occ[q * 16 + lax.rem(zl + block, NZL) * 4 + x]
            denom[block * 128 + q * 16 : block * 128 + q * 16 + 16, :] = ((e_i + e_j) - e_a) - e_b
    v1_step(1)
    slab_step(2)
    t_copy(0, 1).wait_recv()
    go(t_sibling(3, 1))
    t_copy(1, 0).wait_recv()
    go(t_sibling(1, 0))
    m = lax.broadcasted_iota(jnp.int32, (512, 512), 0)
    n = lax.broadcasted_iota(jnp.int32, (512, 512), 1)
    hit = jnp.logical_and((m >> 4 & 7) == n >> 6, m >> 7 == (n >> 4 & 3))
    hit = jnp.logical_and(hit, (m & 15) == (n & 15))
    order[...] = jnp.where(hit, 1.0, 0.0).astype(jnp.bfloat16)

    v0_x(0, 0).wait_recv()
    go(v0_f(0))
    v0_x(1, 1).wait_recv()
    go(v0_f(1))
    slab_step(3)
    v1_step(2)
    w_load.wait()
    zmat = None
    for c in range(CW):
        rows = w_own[:, c, pl.ds(pl.multiple_of(blk_b * 16, 16), 16), :].reshape(256, NO)
        part = dot(rows, a_mat[c])
        zmat = part if zmat is None else zmat + part
    for block in range(4):
        zs[block] = zmat[:, block * 128 : block * 128 + 128]
    chunk = lax.broadcasted_iota(jnp.int32, (16, 128), 1) >> 4

    def crossed(block, carry):
        for h in range(2):
            outs = [jnp.zeros((16, 128), jnp.float32)] * 8
            for b in range(8):
                part = zs[block, pl.ds(h * 8 + b, 16, stride=16), :]
                for q in range(8):
                    moved = pltpu.roll(part, (b - q) % 8 * 16, 1) if b != q else part
                    outs[q] = jnp.where(chunk == b, -moved, outs[q])
            for q in range(8):
                acc[h, pl.ds(pl.multiple_of(block * 128 + q * 16, 16), 16), :] = outs[q]
        return carry

    lax.fori_loop(0, 4, crossed, 0)

    v0_x(0, 1).wait_recv()
    v0_x(1, 0).wait_recv()
    for d in range(2):
        v0_f(d).wait_recv()
    v1_step(3)
    for slot in range(NX):
        join([s1.at[q, slot] for q in range(NY)], pl.ds(slot * 64 + 32, 32))
    for d in range(2):
        t_forward(d).wait_recv()
        go(t_sibling(2, d))
    for block in (3, 1):
        for h in range(2):
            t_sibling(block, h).wait_recv()

    def ladder(blocks, i):
        ks = pl.ds(pl.multiple_of(i * 768, 768), 768)
        for first_block, n in blocks:
            rows = pl.ds(first_block * 128, n * 128)
            both = dot(t_all[pl.ds(first_block * 8, n * 8), :, ks].reshape(n * 128, 768), v_all[:, ks], NT)
            for h in range(2):
                acc[h, rows, :] += both[:, h * 128 : h * 128 + 128]

    def ladder_most(i, carry):
        ladder(((0, 2), (3, 1)), i)
        return carry

    def ladder_last(i, carry):
        ladder(((2, 1),), i)
        return carry

    lax.fori_loop(0, KK // 768, ladder_most, 0)
    for h in range(2):
        t_sibling(2, h).wait_recv()
    lax.fori_loop(0, KK // 768, ladder_last, 0)

    def near(n):
        return lax.rem(zl + n, NZL)

    for half in range(2):
        for sj in (2 * half, 2 * half + 1):
            for si in range(4):
                for xj in range(4):
                    for h in range(2):
                        mail[pl.ds(xj * 256 + (sj * 4 + si) * 2 + h, 8, stride=32), :] = acc[
                            h, pl.ds(si * 128 + near(sj) * 4 + xj, 8, stride=16), :
                        ]

        def send_mail(n, carry):
            px, py = partner(n)
            src = mail.at[pl.ds(pl.multiple_of((px * 8 + py) * 32 + half * 16, 16), 16)]
            dst = rec.at[pl.ds(pl.multiple_of((x * 8 + y) * 32 + half * 16, 16), 16)]
            remote(src, dst, m_send.at[half], m_recv.at[half], dev(px, py, z, twin)).start()
            return carry

        lax.fori_loop(first, 32, send_mail, 0)

        @pl.when(diag)
        def _():
            here = pl.ds(pl.multiple_of((x * 8 + y) * 32 + half * 16, 16), 16)
            pltpu.make_async_copy(mail.at[here], rec.at[here], m_recv.at[half]).start()

    owner_z = lax.div(blk_a, 2) * NZL
    owner_k = lax.rem(blk_a, 2)

    for block in range(4):
        rows = pl.ds(block * 128, 128)
        turned = None
        for h in range(2):
            part = acc[h, rows, :]
            hi = part.astype(jnp.bfloat16)
            rest = part - hi.astype(jnp.float32)
            mid = rest.astype(jnp.bfloat16)
            low = (rest - mid.astype(jnp.float32)).astype(jnp.bfloat16)
            matrix = swap[h * 128 : h * 128 + 128, :]
            term = dot(hi, matrix) + (dot(mid, matrix) + dot(low, matrix))
            turned = term if turned is None else turned + term
        for h in range(2):
            own_x[h, rows, :] = turned[:, h * 128 : h * 128 + 128]

    for half in range(2):
        some = rec.at[pl.ds(0, 512)]
        pltpu.make_async_copy(some, some, m_recv.at[half]).wait()
        for sj in (2 * half, 2 * half + 1):
            for si in range(4):
                for xj in range(4):
                    for h in range(2):
                        rows = pl.ds(sj * 128 + near(si) * 4 + xj, 8, stride=16)
                        own_x[h, rows, :] += rec[pl.ds(xj * 256 + (sj * 4 + si) * 2 + h, 8, stride=32), :]
        for sj in (2 * half, 2 * half + 1):
            rows = pl.ds(sj * 128, 128)
            for h in range(2):
                lanes = pl.ds(h * 128, 128)
                sbuf[rows, lanes] = (own_x[h, rows, :] / denom[rows, lanes]).astype(jnp.bfloat16)
            target = owner_z + near(sj)
            n = sem("d", sj)
            if sj == 0:

                @pl.when(own)
                def _():
                    pltpu.make_async_copy(sbuf.at[rows], d_all.at[blk_b], d_recv).start()

                @pl.when(jnp.logical_not(own))
                def _():
                    remote(sbuf.at[rows], d_all.at[blk_b], ssem.at[n], d_recv, dev(x, y, target, owner_k)).start()
            else:
                go(remote(sbuf.at[rows], d_all.at[blk_b], ssem.at[n], d_recv, dev(x, y, target, owner_k)))

    pltpu.make_async_copy(d_all, d_all, d_recv).wait()
    for h in range(2):
        some = jnp.concatenate([d_all[b, :, h * 128 : h * 128 + 128] for b in range(4)], axis=1)
        out_ref[:, h * 512 : h * 512 + 512] = dot(some, order[...]).astype(jnp.bfloat16)

    for copy in sends:
        copy.wait_send()

    @pl.when(moves)
    def _():
        for src, dst, n in raw:
            pltpu.make_async_copy(src, src, ssem.at[n]).wait()

    @pl.when(jnp.logical_not(own))
    def _():
        some = sbuf.at[pl.ds(0, 128)]
        pltpu.make_async_copy(some, some, ssem.at[sem("d", 0)]).wait()

    three = a_mat.at[:, pl.ds(0, 16), pl.ds(0, 384)]

    @pl.when(own)
    def _():
        pltpu.make_async_copy(three, three, a_send).wait()

    @pl.when(jnp.logical_not(own))
    def _():
        pltpu.make_async_copy(slab_rows, slab_rows, a_send).wait()

    @pl.when(diag)
    def _():
        for half in range(2):
            some = rec.at[pl.ds(0, 31 * 16)]
            pltpu.make_async_copy(some, some, m_send.at[half]).wait()

    @pl.when(jnp.logical_not(diag))
    def _():
        for half in range(2):
            some = rec.at[pl.ds(0, 512)]
            pltpu.make_async_copy(some, some, m_send.at[half]).wait()


def call(t, vv, w, irreps, occ, vir):
    bf, f32 = jnp.bfloat16, jnp.float32
    vm = pl.BlockSpec(memory_space=pltpu.VMEM)
    smem = pl.BlockSpec(memory_space=pltpu.SMEM)
    anywhere = pl.BlockSpec(memory_space=pl.ANY)
    dma = pltpu.SemaphoreType.DMA
    return pl.pallas_call(
        kernel,
        out_shape=jax.ShapeDtypeStruct((NO, 1024), bf),
        in_specs=[anywhere, vm, anywhere, smem, smem, smem],
        out_specs=vm,
        scratch_shapes=[
            pltpu.VMEM((32, 16, KK), bf),
            pltpu.VMEM((NY, 32, PIECE), bf),
            pltpu.VMEM((NY, NX, 32, PIECE), bf),
            pltpu.VMEM((256, KK), bf),
            pltpu.VMEM((CW, NO, 512), bf),
            pltpu.VMEM((4, 256, 128), f32),
            pltpu.VMEM((2, 512, 128), f32),
            pltpu.VMEM((2, 512, 128), f32),
            pltpu.VMEM((512, 512), bf),
            pltpu.VMEM((256, 256), bf),
            pltpu.VMEM((1024, 128), bf),
            pltpu.VMEM((CW, 16, 128), bf),
            pltpu.VMEM((64, PIECE), bf),
            pltpu.VMEM((16, CW, SA, NO), bf),
            pltpu.VMEM((512, 256), f32),
            pltpu.VMEM((1024, 128), f32),
            pltpu.VMEM((1024, 128), f32),
            pltpu.VMEM((512, 256), bf),
            pltpu.VMEM((4, 128, 256), bf),
            dma((80,)), dma((80,)), dma((4,)), dma, dma, dma((2,)), dma((2,)), dma,
        ],
        compiler_params=pltpu.CompilerParams(
            collective_id=0, has_side_effects=True, vmem_limit_bytes=64 * 1024 * 1024
        ),
        cost_estimate=pl.CostEstimate(flops=2 * 512 * 256 * KK, bytes_accessed=20_000_000, transcendentals=0),
    )(t, vv, w, irreps, occ, vir)


def local(amplitudes, integrals, hole_integrals, irreps, occ_energy, vir_energy):
    t = jnp.transpose(amplitudes.reshape(8, 16, CW, NV), (0, 2, 1, 3))
    vv = jnp.transpose(integrals, (1, 0, 2, 3)).reshape(64, CW, DW)
    vv = jnp.pad(vv, ((0, 0), (0, 0), (0, 256 - DW))).reshape(64, PIECE)
    w = jnp.transpose(hole_integrals.reshape(NO, 16, CW, SA), (1, 2, 3, 0))
    out = call(t, vv, w, irreps, occ_energy, vir_energy)
    return out.reshape(8, 1, 1, 1, 16, 16, SA)


def solution(mesh):
    in_specs = (
        P(None, "row", None, "col", None, None, None),
        P("vir", "row", None, "col"),
        P(None, None, "col", None, None, None),
        P(),
        P(),
        P(),
    )
    out_specs = P(None, "row", None, "col", None, "vir", None)
    return jax.shard_map(local, mesh=mesh, in_specs=in_specs, out_specs=out_specs, check_vma=False)
```

time: 290 us -> 84.8 us (0.29)
  waiting for transfers between devices: 125 us -> 0 us
  blocking collectives: 107 us -> 0 us
  Pallas kernels: 0 us -> 80.8 us
  local copies, waits for them, and re-layouts: 26.1 us -> 3.84 us
  between operations: 13.6 us -> 0.03 us
  starting transfers between devices: 8.58 us -> 0 us
  matrix products: 6.9 us -> 0 us
    all_gather x1 -> x0, waiting for transfers between devices: 111 us -> none  [local(): piece = lax.all_gather(full_d, 'row', axis=1, tiled=True)]
    pallas_call x0 -> x1, Pallas kernels: none -> 80.8 us  [call(): pl.pallas_call(kernel, out_shape=jax.ShapeDtypeStruct((NO, 1024), bf), in...]
    all_gather x2 -> x0, blocking collectives: 78.2 us -> none  [the longest x1 54.8 us: local(): full_d = lax.all_gather(integrals, 'col', axis=3, tiled=True)]
    all_to_all x1 -> x0, blocking collectives: 28.9 us -> none  [local(): lax.all_to_all(outgoing, ('row', 'col'), split_axis=0, concat_axis=0, til...]
    all_to_all x1 -> x0, waiting for transfers between devices: 13.6 us -> none  [local(): lax.all_to_all(lax.all_to_all(outgoing, ('row', 'col'), split_axis=0, con...]
    all_to_all x1 -> x0, starting transfers between devices: 8.58 us -> none  [local(): lax.all_to_all(lax.all_to_all(outgoing, ('row', 'col'), split_axis=0, con...]
    all_gather x2 -> x0, local copies, waits for them, and re-layouts: 8.13 us -> none  [the longest x1 7.66 us: local(): full_d = lax.all_gather(integrals, 'col', axis=3, tiled=True)]
    dot_general x2 -> x0, matrix products: 6.9 us -> none  [the longest x1 6.25 us: contract(): lax.dot_general(amp_rows, block, (((1, 2), (2, 3)), ((), ())), preferred_...]
  transfers between devices with their start and end apart: 2 -> 0, of which waited for: 2 -> 0; matrix products, arithmetic and copies ran while one was open for 2% -> 0% of each run, Pallas kernels for 0% -> 0%
where the time goes in v2:
time: 84.8 us; the launch traced here: 84.6 us
  Pallas kernels  80.8 us (95%)
  local copies, waits for them, and re-layouts  3.84 us (5%)
    pallas_call x1, Pallas kernels, call(): pl.pallas_call(kernel, out_shape=jax.ShapeDtypeStruct((NO, 1024), bf), in...  80.8 us
    reshape x1, local copies, waits for them, and re-layouts, local(): return out.reshape(8, 1, 1, 1, 16, 16, SA)  2.13 us

profile of v2, /device:TPU:1, one launch (start us, length us, event | category | flops | bytes accessed | tf_op | source)
XLA Modules:
  0.0 84.6 jit_solution(1328034306392377845)
XLA Ops:
  0.0 0.9 %copy.8 = bf16[16,4,3,224]{3,0,1,2:T(8,128)(2,1)S(1)} copy(bf16[16,4,3,224]{3,1,2,0:T(4,128)(2,1)} %param.7) | data formatting | bytes 172032 | tf_op args[1]
  0.9 0.1 copy.11
  1.0 0.1 pad.4.clone
  1.1 0.7 copy.12
  1.7 80.8 %shard_map.64 = bf16[128,1024]{1,0:T(8,128)(2,1)} custom-call(bf16[8,3,16,1792]{3,2,1,0:T(8,128)(2,1)} %bitcast.15, bf16[64,768]{1,0:T(8,128)(2,1)} %bitcast.14, bf16[16,3,64,128]{3,2,1,0:T(8,128)(2,1)} %bitcast.16, s32[112]{0:T(128)} %irreps.1, f32[128]{0:T(128)} %occ.1, f32[64]{0:T(128)} %vir.1), custom_call_target="tpu_custom_call" | custom-call | flops 1409286144 | bytes 20000000 | tf_op jit(solution)/shard_map/pallas_call | solution.py:508
  82.5 2.1 %reshape.19 = bf16[8,1,1,1,16,16,64]{6,5,4,0,3,2,1:T(8,128)(2,1)} reshape(bf16[128,1024]{1,0:T(8,128)(2,1)} %shard_map.64) | data formatting | bytes 524288 | tf_op jit(solution)/shard_map/reshape | solution.py:548

commit v3 on v2

--- a/solution.py
+++ b/solution.py
@@ -22,6 +22,7 @@
     (0, 1), (1, 0), (0, 0), (1, 1), (2, 1), (1, 2), (0, 3), (3, 0),
     (2, 0), (0, 2), (1, 3), (3, 1), (2, 2), (3, 3), (2, 3), (3, 2),
 ]
+ABOVE = (0, 3, 1, 2)
 PLACE_OF = [WORK.index((a, b)) for a in range(4) for b in range(4)]
 
 
@@ -100,14 +101,16 @@
     first = jnp.where(diag, 1, 0)
 
     def partner(n):
-        return (lax.rem(x + lax.rem(n, NX), NX), lax.rem(y + lax.div(n, NX), NY))
+        m = lax.div(n, NX)
+        far = jnp.where(lax.rem(m, 2) == 1, 4 - lax.div(m + 1, 2), 4 + lax.div(m, 2))
+        return (lax.rem(x + 3 - lax.rem(n, NX), NX), lax.rem(y + far, NY))
 
     def greet_mail(n, carry):
         px, py = partner(n)
         greet(dev(px, py, z, twin))
         return carry
 
-    lax.fori_loop(first, 32, greet_mail, 0)
+    lax.fori_loop(0, 32 - first, greet_mail, 0)
     label = jnp.bitwise_xor(jnp.bitwise_xor(irreps[v], irreps[zl]), irreps[0])
     lane = lax.broadcasted_iota(jnp.int32, (8, PIECE), 1) & 255
     kept = jnp.zeros((8, PIECE), jnp.float32)
@@ -122,9 +125,14 @@
     pull[...] = jnp.where(hit, 1.0, 0.0).astype(jnp.bfloat16)
     for load in t_loads:
         load.wait()
-    for c in range(CW):
-        wide = jnp.concatenate([t_all[q, :, c * NV : c * NV + 128] for q in range(8)], axis=1)
-        a_own[c] = dot(wide, pull[...]).astype(jnp.bfloat16)
+    wide = jnp.concatenate(
+        [
+            jnp.concatenate([t_all[q, :, c * NV : c * NV + 128] for q in range(8)], axis=1)
+            for c in range(CW)
+        ],
+        axis=0,
+    )
+    a_own[...] = dot(wide, pull[...]).astype(jnp.bfloat16).reshape(CW, 16, 128)
     pl.semaphore_wait(barrier, 3 + 7 + 15 + 32 - first)
 
     names = {}
@@ -141,19 +149,37 @@
         copy.start()
         sends.append(copy)
 
-    t_block = (3, 1)
-
-    def t_rows(block, h):
-        return t_all.at[pl.ds(block * 8 + k * 4 + h * 2, 2)]
-
-    def t_copy(d, h):
-        return hop(t_rows(0, h), t_rows(t_block[d], h), dev(x, y, zn[d], k), "t", d, h)
-
-    def t_forward(d):
-        return hop(t_rows(t_block[d], d), t_rows(2, d), dev(x, y, zn[d], k), "tf", d)
-
-    def t_sibling(block, h):
-        return hop(t_rows(block, h), t_rows(block, h), dev(x, y, z, 1 - k), "ts", block, h)
+    t_block = (1, 2)
+
+    def t_rows(block, u):
+        return t_all.at[pl.ds(block * 8 + k * 4 + u, 1)]
+
+    def t_copy(d, i):
+        u = 3 * d + (1 - 2 * d) * i
+        return hop(t_rows(0, u), t_rows(t_block[d], u), dev(x, y, zn[d], k), "t", d, i)
+
+    def t_forward(d, i):
+        u = 3 * d + (1 - 2 * d) * i
+        return hop(t_rows(t_block[d], u), t_rows(3, u), dev(x, y, zn[d], k), "tf", d, i)
+
+    def t_sibling(block, u):
+        return hop(t_rows(block, u), t_rows(block, u), dev(x, y, z, 1 - k), "ts", block, u)
+
+    def t_start(i):
+        for d in range(2):
+            go(t_copy(d, i))
+
+    def t_step(i):
+        for d in range(2):
+            t_copy(d, i).wait_recv()
+            if i < 2:
+                go(t_forward(d, i))
+            go(t_sibling(t_block[d], 3 * d + (1 - 2 * d) * i))
+
+    def t_last(i):
+        for d in range(2):
+            t_forward(d, i).wait_recv()
+            go(t_sibling(3, 3 * d + (1 - 2 * d) * i))
 
     def slab_place(block):
         rows = pl.ds(pl.multiple_of(y * 16, 16), 16)
@@ -210,7 +236,8 @@
     for b in range(4):
         at = pick(v * 4 + b, PLACE_OF)
         az, ak = lax.div(at, 2), lax.rem(at, 2)
-        block = lax.rem(zl - lax.rem(az, NZL) + NZL, NZL)
+        above = lax.rem(zl - lax.rem(az, NZL) + NZL, NZL)
+        block = jnp.where(above == 0, 0, jnp.where(above == 3, 1, above + 1))
         mine = at == z * 2 + k
 
         @pl.when(mine)
@@ -221,10 +248,8 @@
         def _():
             remote(a_own, slab_place(block), a_send, a_recv, dev(x, y, az, ak)).start()
 
-    go(t_copy(0, 0))
-    go(t_copy(1, 1))
-    go(t_copy(0, 1))
-    go(t_copy(1, 0))
+    t_start(0)
+    t_start(1)
     for src, dst, n in raw:
         pltpu.make_async_copy(src, dst, rsem.at[n]).wait()
         if n == raw[0][2]:
@@ -258,14 +283,20 @@
             if s < 3 - d:
                 go(slab_y(d, s + 1))
 
-    def join(source, rows):
+    def join(source, rows, half):
         for c in range(CW):
-            for half in range(2):
-                joined = jnp.concatenate(
-                    [source[half * 4 + q][:, c * 256 : c * 256 + DW] for q in range(4)], axis=1
-                )
-                v_all[rows, c * NV + half * 896 : c * NV + (half + 1) * 896] = joined
-
+            joined = jnp.concatenate([source(half * 4 + q, c) for q in range(4)], axis=1)
+            v_all[rows, pl.ds(pl.multiple_of(c * NV + half * 896, 128), 896)] = joined
+
+    def join0(half):
+        rows = pl.ds(pl.multiple_of(x * 64, 32), 32)
+        join(lambda q, c: s0[q, :, c * 256 : c * 256 + DW], rows, half)
+
+    def join1(half):
+        for slot in range(NX):
+            join(lambda q, c: s1[q, slot, :, c * 256 : c * 256 + DW], pl.ds(slot * 64 + 32, 32), half)
+
+    near_half = lax.div(y, 4)
     v0_step(0)
     for n in range(1, NX):
         v1_x(n).wait_recv()
@@ -277,21 +308,19 @@
     go(slab_y(0, 0))
     go(slab_y(1, 0))
     v0_step(2)
-    t_copy(0, 0).wait_recv()
-    go(t_forward(0))
-    go(t_sibling(3, 0))
-    t_copy(1, 1).wait_recv()
-    go(t_forward(1))
-    go(t_sibling(1, 1))
+    t_step(0)
+    t_start(2)
     v1_step(0)
-    slab_step(0)
+    t_step(1)
+    t_start(3)
     v0_step(3)
-    join([s0.at[q] for q in range(NY)], pl.ds(pl.multiple_of(x * 64, 32), 32))
+    for half in range(2):
+        join0(half)
     go(v0_x(0, 0))
     go(v0_x(1, 1))
     go(v0_x(0, 1))
     go(v0_x(1, 0))
-    slab_step(1)
+    slab_step(0)
     m = lax.broadcasted_iota(jnp.int32, (256, 256), 0)
     n = lax.broadcasted_iota(jnp.int32, (256, 256), 1)
     hit = jnp.logical_and(m >> 4 == (n & 15), (m & 15) == n >> 4)
@@ -307,14 +336,10 @@
         e_b = jnp.where((lane & 15) == n, vir[blk_b * 16 + n], e_b)
     for block in range(4):
         for q in range(8):
-            e_i = occ[q * 16 + lax.rem(zl + block, NZL) * 4 + x]
+            e_i = occ[q * 16 + lax.rem(zl + ABOVE[block], NZL) * 4 + x]
             denom[block * 128 + q * 16 : block * 128 + q * 16 + 16, :] = ((e_i + e_j) - e_a) - e_b
     v1_step(1)
-    slab_step(2)
-    t_copy(0, 1).wait_recv()
-    go(t_sibling(3, 1))
-    t_copy(1, 0).wait_recv()
-    go(t_sibling(1, 0))
+    slab_step(1)
     m = lax.broadcasted_iota(jnp.int32, (512, 512), 0)
     n = lax.broadcasted_iota(jnp.int32, (512, 512), 1)
     hit = jnp.logical_and((m >> 4 & 7) == n >> 6, m >> 7 == (n >> 4 & 3))
@@ -325,8 +350,10 @@
     go(v0_f(0))
     v0_x(1, 1).wait_recv()
     go(v0_f(1))
+    slab_step(2)
+    t_step(2)
+    v1_step(2)
     slab_step(3)
-    v1_step(2)
     w_load.wait()
     zmat = None
     for c in range(CW):
@@ -351,70 +378,74 @@
 
     lax.fori_loop(0, 4, crossed, 0)
 
+    t_step(3)
+    t_last(0)
     v0_x(0, 1).wait_recv()
     v0_x(1, 0).wait_recv()
     for d in range(2):
         v0_f(d).wait_recv()
+    join1(near_half)
     v1_step(3)
-    for slot in range(NX):
-        join([s1.at[q, slot] for q in range(NY)], pl.ds(slot * 64 + 32, 32))
-    for d in range(2):
-        t_forward(d).wait_recv()
-        go(t_sibling(2, d))
-    for block in (3, 1):
-        for h in range(2):
-            t_sibling(block, h).wait_recv()
-
-    def ladder(blocks, i):
-        ks = pl.ds(pl.multiple_of(i * 768, 768), 768)
-        for first_block, n in blocks:
-            rows = pl.ds(first_block * 128, n * 128)
-            both = dot(t_all[pl.ds(first_block * 8, n * 8), :, ks].reshape(n * 128, 768), v_all[:, ks], NT)
+    t_last(1)
+    join1(1 - near_half)
+    for u in range(4):
+        t_sibling(1, u).wait_recv()
+
+    def ladder(pair):
+        def step(i, carry):
+            ks = pl.ds(pl.multiple_of(i * 1792, 1792), 1792)
+            both = dot(t_all[pl.ds(pair * 16, 16), :, ks].reshape(256, 1792), v_all[:, ks], NT)
             for h in range(2):
-                acc[h, rows, :] += both[:, h * 128 : h * 128 + 128]
-
-    def ladder_most(i, carry):
-        ladder(((0, 2), (3, 1)), i)
-        return carry
-
-    def ladder_last(i, carry):
-        ladder(((2, 1),), i)
-        return carry
-
-    lax.fori_loop(0, KK // 768, ladder_most, 0)
-    for h in range(2):
-        t_sibling(2, h).wait_recv()
-    lax.fori_loop(0, KK // 768, ladder_last, 0)
+                acc[h, pl.ds(pair * 256, 256), :] += both[:, h * 128 : h * 128 + 128]
+            return carry
+
+        lax.fori_loop(0, KK // 1792, step, 0)
 
     def near(n):
-        return lax.rem(zl + n, NZL)
-
-    for half in range(2):
-        for sj in (2 * half, 2 * half + 1):
-            for si in range(4):
+        return lax.rem(zl + ABOVE[n], NZL)
+
+    def tile_row(si, sj, h):
+        return (si // 2 * 2 + sj // 2) * 8 + (si % 2 * 2 + sj % 2) * 2 + h
+
+    def fill(pair, half):
+        for si in (2 * pair, 2 * pair + 1):
+            for sj in (2 * half, 2 * half + 1):
                 for xj in range(4):
                     for h in range(2):
-                        mail[pl.ds(xj * 256 + (sj * 4 + si) * 2 + h, 8, stride=32), :] = acc[
+                        mail[pl.ds(xj * 256 + tile_row(si, sj, h), 8, stride=32), :] = acc[
                             h, pl.ds(si * 128 + near(sj) * 4 + xj, 8, stride=16), :
                         ]
 
+    def post(part, start, rows):
         def send_mail(n, carry):
             px, py = partner(n)
-            src = mail.at[pl.ds(pl.multiple_of((px * 8 + py) * 32 + half * 16, 16), 16)]
-            dst = rec.at[pl.ds(pl.multiple_of((x * 8 + y) * 32 + half * 16, 16), 16)]
-            remote(src, dst, m_send.at[half], m_recv.at[half], dev(px, py, z, twin)).start()
+            src = mail.at[pl.ds(pl.multiple_of((px * 8 + py) * 32 + start, 8), rows)]
+            dst = rec.at[pl.ds(pl.multiple_of((x * 8 + y) * 32 + start, 8), rows)]
+            remote(src, dst, m_send.at[part], m_recv.at[part], dev(px, py, z, twin)).start()
             return carry
 
-        lax.fori_loop(first, 32, send_mail, 0)
+        lax.fori_loop(0, 32 - first, send_mail, 0)
 
         @pl.when(diag)
         def _():
-            here = pl.ds(pl.multiple_of((x * 8 + y) * 32 + half * 16, 16), 16)
-            pltpu.make_async_copy(mail.at[here], rec.at[here], m_recv.at[half]).start()
+            here = pl.ds(pl.multiple_of((x * 8 + y) * 32 + start, 8), rows)
+            pltpu.make_async_copy(mail.at[here], rec.at[here], m_recv.at[part]).start()
+
+    ladder(0)
+    fill(0, 0)
+    fill(0, 1)
+    post(0, 0, 16)
+    for block in (2, 3):
+        for u in range(4):
+            t_sibling(block, u).wait_recv()
+    ladder(1)
+    fill(1, 0)
+    post(1, 16, 8)
+    fill(1, 1)
+    post(2, 24, 8)
 
     owner_z = lax.div(blk_a, 2) * NZL
     owner_k = lax.rem(blk_a, 2)
-
     for block in range(4):
         rows = pl.ds(block * 128, 128)
         turned = None
@@ -430,15 +461,24 @@
         for h in range(2):
             own_x[h, rows, :] = turned[:, h * 128 : h * 128 + 128]
 
-    for half in range(2):
-        some = rec.at[pl.ds(0, 512)]
-        pltpu.make_async_copy(some, some, m_recv.at[half]).wait()
-        for sj in (2 * half, 2 * half + 1):
-            for si in range(4):
+    def arrived(part, count):
+        some = rec.at[pl.ds(0, count)]
+        pltpu.make_async_copy(some, some, m_recv.at[part]).wait()
+
+    def take(pair, half):
+        for si in (2 * pair, 2 * pair + 1):
+            for sj in (2 * half, 2 * half + 1):
                 for xj in range(4):
                     for h in range(2):
                         rows = pl.ds(sj * 128 + near(si) * 4 + xj, 8, stride=16)
-                        own_x[h, rows, :] += rec[pl.ds(xj * 256 + (sj * 4 + si) * 2 + h, 8, stride=32), :]
+                        own_x[h, rows, :] += rec[pl.ds(xj * 256 + tile_row(si, sj, h), 8, stride=32), :]
+
+    arrived(0, 512)
+    take(0, 0)
+    take(0, 1)
+    for half in range(2):
+        arrived(1 + half, 256)
+        take(1, half)
         for sj in (2 * half, 2 * half + 1):
             rows = pl.ds(sj * 128, 128)
             for h in range(2):
@@ -486,17 +526,17 @@
     def _():
         pltpu.make_async_copy(slab_rows, slab_rows, a_send).wait()
 
-    @pl.when(diag)
-    def _():
-        for half in range(2):
-            some = rec.at[pl.ds(0, 31 * 16)]
-            pltpu.make_async_copy(some, some, m_send.at[half]).wait()
-
-    @pl.when(jnp.logical_not(diag))
-    def _():
-        for half in range(2):
-            some = rec.at[pl.ds(0, 512)]
-            pltpu.make_async_copy(some, some, m_send.at[half]).wait()
+    for part, rows in ((0, 16), (1, 8), (2, 8)):
+
+        @pl.when(diag)
+        def _():
+            some = rec.at[pl.ds(0, 31 * rows)]
+            pltpu.make_async_copy(some, some, m_send.at[part]).wait()
+
+        @pl.when(jnp.logical_not(diag))
+        def _():
+            some = rec.at[pl.ds(0, 32 * rows)]
+            pltpu.make_async_copy(some, some, m_send.at[part]).wait()
 
 
 def call(t, vv, w, irreps, occ, vir):
@@ -530,7 +570,7 @@
             pltpu.VMEM((1024, 128), f32),
             pltpu.VMEM((512, 256), bf),
             pltpu.VMEM((4, 128, 256), bf),
-            dma((80,)), dma((80,)), dma((4,)), dma, dma, dma((2,)), dma((2,)), dma,
+            dma((96,)), dma((96,)), dma((4,)), dma, dma, dma((3,)), dma((3,)), dma,
         ],
         compiler_params=pltpu.CompilerParams(
             collective_id=0, has_side_effects=True, vmem_limit_bytes=64 * 1024 * 1024

time: 84.8 us -> 78.5 us (0.926)
  Pallas kernels: 80.8 us -> 74.4 us
    pallas_call x1, Pallas kernels: 80.8 us -> 74.4 us  [call(): pl.pallas_call(kernel, out_shape=jax.ShapeDtypeStruct((NO, 1024), bf), in...]
where the time goes in v3:
time: 78.5 us; the launch traced here: 78.3 us
  Pallas kernels  74.4 us (95%)
  local copies, waits for them, and re-layouts  3.84 us (5%)
    pallas_call x1, Pallas kernels, call(): pl.pallas_call(kernel, out_shape=jax.ShapeDtypeStruct((NO, 1024), bf), in...  74.4 us
    reshape x1, local copies, waits for them, and re-layouts, local(): return out.reshape(8, 1, 1, 1, 16, 16, SA)  2.13 us
    unnamed x3, local copies, waits for them, and re-layouts  1.64 us

profile of v3, /device:TPU:1, one launch (start us, length us, event | category | flops | bytes accessed | tf_op | source)
XLA Modules:
  0.0 78.3 jit_solution(935355969478489248)
XLA Ops:
  0.0 0.9 %copy.8 = bf16[16,4,3,224]{3,0,1,2:T(8,128)(2,1)S(1)} copy(bf16[16,4,3,224]{3,1,2,0:T(4,128)(2,1)} %param.7) | data formatting | bytes 172032 | tf_op args[1]
  0.9 0.1 copy.11
  1.0 0.1 pad.4.clone
  1.1 0.7 copy.12
  1.7 74.4 %shard_map.64 = bf16[128,1024]{1,0:T(8,128)(2,1)} custom-call(bf16[8,3,16,1792]{3,2,1,0:T(8,128)(2,1)} %bitcast.15, bf16[64,768]{1,0:T(8,128)(2,1)} %bitcast.14, bf16[16,3,64,128]{3,2,1,0:T(8,128)(2,1)} %bitcast.16, s32[112]{0:T(128)} %irreps.1, f32[128]{0:T(128)} %occ.1, f32[64]{0:T(128)} %vir.1), custom_call_target="tpu_custom_call" | custom-call | flops 1409286144 | bytes 20000000 | tf_op jit(solution)/shard_map/pallas_call | solution.py:548
  76.1 2.1 %reshape.19 = bf16[8,1,1,1,16,16,64]{6,5,4,0,3,2,1:T(8,128)(2,1)} reshape(bf16[128,1024]{1,0:T(8,128)(2,1)} %shard_map.64) | data formatting | bytes 524288 | tf_op jit(solution)/shard_map/reshape | solution.py:588

commit v4 on v3

--- a/solution.py
+++ b/solution.py
@@ -49,7 +49,7 @@
 
 def kernel(
     t_ref, v_ref, w_ref, irreps, occ, vir, out_ref,
-    t_all, s0, s1, v_all, a_mat, zs, acc, own_x, order, swap, pull, a_own, v_own, w_own, denom, mail, rec, sbuf, d_all,
+    t_all, s0, x1, s1, v_all, a_mat, zs, acc, own_x, order, swap, pull, a_own, v_raw, v_own, w_own, denom, mail, rec, sbuf, d_all,
     ssem, rsem, load_sem, a_send, a_recv, m_send, m_recv, d_recv,
 ):
     r = lax.axis_index("row")
@@ -77,6 +77,8 @@
     for load in t_loads:
         load.start()
     w_load.start()
+    v_load = pltpu.make_async_copy(v_ref, v_raw, load_sem.at[4])
+    v_load.start()
 
     barrier = pltpu.get_barrier_semaphore()
 
@@ -117,7 +119,12 @@
     for n in range(DW // VBLK):
         same = jnp.where(irreps[y * (DW // VBLK) + n] == label, 1.0, 0.0)
         kept = jnp.where(lane >> 4 == n, same, kept)
-    v_own[...] = (v_ref[...].astype(jnp.float32) * kept[0:1]).astype(jnp.bfloat16)
+    v_own[...] = jnp.zeros_like(v_own)
+    v_load.wait()
+    for b in range(4):
+        for c in range(CW):
+            part = v_raw[:, c, b, :].astype(jnp.float32) * kept[0:1, :DW]
+            v_own[b * 16 : b * 16 + 16, c * 256 : c * 256 + DW] = part.astype(jnp.bfloat16)
 
     m = lax.broadcasted_iota(jnp.int32, (1024, 128), 0)
     n = lax.broadcasted_iota(jnp.int32, (1024, 128), 1)
@@ -208,11 +215,12 @@
         return hop(rows, rows, dev(xs[d], y, z, k), "v0f", d)
 
     def v1_x(n):
-        slot = s1.at[y, x]
+        slot = x1.at[x]
         return hop(slot, slot, dev(lax.rem(x + n, NX), y, z, k), "v1x", n)
 
     def v1_y(d, s, e):
-        slot = s1.at[lax.rem(y + (NY - s if d == 0 else s), NY), pl.ds(2 * e, 2)]
+        lanes = pl.ds(1408 * e, 1408 - 128 * e)
+        slot = s1.at[lax.rem(y + (NY - s if d == 0 else s), NY), :, lanes]
         return hop(slot, slot, dev(x, ys[d], z, k), "v1y", d, s, e)
 
     there = pick(v * 4 + zl, PLACE_OF)
@@ -220,7 +228,7 @@
     go_there = dev(x, y, lax.div(there, 2), lax.rem(there, 2))
     raw = [
         (v_own.at[pl.ds(0, 32)], s0.at[y], sem("r", 0)),
-        (v_own.at[pl.ds(32, 32)], s1.at[y, x], sem("r", 1)),
+        (v_own.at[pl.ds(32, 32)], x1.at[x], sem("r", 1)),
     ]
 
     @pl.when(moves)
@@ -294,12 +302,28 @@
 
     def join1(half):
         for slot in range(NX):
-            join(lambda q, c: s1[q, slot, :, c * 256 : c * 256 + DW], pl.ds(slot * 64 + 32, 32), half)
+            first_lane = slot * CW * DW
+            join(
+                lambda q, c: s1[q, :, first_lane + c * DW : first_lane + c * DW + DW],
+                pl.ds(slot * 64 + 32, 32),
+                half,
+            )
 
     near_half = lax.div(y, 4)
+
+    def ladder(pair, half):
+        for c in range(CW):
+            ks = pl.ds(pl.multiple_of(c * NV + half * 896, 128), 896)
+            both = dot(t_all[pl.ds(pair * 16, 16), :, ks].reshape(256, 896), v_all[:, ks], NT)
+            for h in range(2):
+                acc[h, pl.ds(pair * 256, 256), :] += both[:, h * 128 : h * 128 + 128]
+
     v0_step(0)
     for n in range(1, NX):
         v1_x(n).wait_recv()
+    s1[y] = jnp.concatenate(
+        [x1[slot, :, c * 256 : c * 256 + DW] for slot in range(NX) for c in range(CW)], axis=1
+    )
     for e in range(2):
         go(v1_y(0, 0, e))
         go(v1_y(1, 0, e))
@@ -385,22 +409,11 @@
     for d in range(2):
         v0_f(d).wait_recv()
     join1(near_half)
-    v1_step(3)
-    t_last(1)
-    join1(1 - near_half)
     for u in range(4):
         t_sibling(1, u).wait_recv()
-
-    def ladder(pair):
-        def step(i, carry):
-            ks = pl.ds(pl.multiple_of(i * 1792, 1792), 1792)
-            both = dot(t_all[pl.ds(pair * 16, 16), :, ks].reshape(256, 1792), v_all[:, ks], NT)
-            for h in range(2):
-                acc[h, pl.ds(pair * 256, 256), :] += both[:, h * 128 : h * 128 + 128]
-            return carry
-
-        lax.fori_loop(0, KK // 1792, step, 0)
-
+    ladder(0, near_half)
+    v1_step(3)
+    join1(1 - near_half)
     def near(n):
         return lax.rem(zl + ABOVE[n], NZL)
 
@@ -431,14 +444,16 @@
             here = pl.ds(pl.multiple_of((x * 8 + y) * 32 + start, 8), rows)
             pltpu.make_async_copy(mail.at[here], rec.at[here], m_recv.at[part]).start()
 
-    ladder(0)
+    ladder(0, 1 - near_half)
     fill(0, 0)
     fill(0, 1)
     post(0, 0, 16)
+    t_last(1)
     for block in (2, 3):
         for u in range(4):
             t_sibling(block, u).wait_recv()
-    ladder(1)
+    for half in range(2):
+        ladder(1, half)
     fill(1, 0)
     post(1, 16, 8)
     fill(1, 1)
@@ -490,18 +505,22 @@
 
                 @pl.when(own)
                 def _():
-                    pltpu.make_async_copy(sbuf.at[rows], d_all.at[blk_b], d_recv).start()
+                    pltpu.make_async_copy(sbuf.at[rows], d_all.at[blk_b], d_recv.at[blk_b]).start()
 
                 @pl.when(jnp.logical_not(own))
                 def _():
-                    remote(sbuf.at[rows], d_all.at[blk_b], ssem.at[n], d_recv, dev(x, y, target, owner_k)).start()
+                    remote(sbuf.at[rows], d_all.at[blk_b], ssem.at[n], d_recv.at[blk_b], dev(x, y, target, owner_k)).start()
             else:
-                go(remote(sbuf.at[rows], d_all.at[blk_b], ssem.at[n], d_recv, dev(x, y, target, owner_k)))
-
-    pltpu.make_async_copy(d_all, d_all, d_recv).wait()
+                go(remote(sbuf.at[rows], d_all.at[blk_b], ssem.at[n], d_recv.at[blk_b], dev(x, y, target, owner_k)))
+
+    parts = [None, None]
+    for b in range(4):
+        pltpu.make_async_copy(d_all.at[b], d_all.at[b], d_recv.at[b]).wait()
+        for h in range(2):
+            term = dot(d_all[b, :, h * 128 : h * 128 + 128], order[b * 128 : b * 128 + 128, :])
+            parts[h] = term if b == 0 else parts[h] + term
     for h in range(2):
-        some = jnp.concatenate([d_all[b, :, h * 128 : h * 128 + 128] for b in range(4)], axis=1)
-        out_ref[:, h * 512 : h * 512 + 512] = dot(some, order[...]).astype(jnp.bfloat16)
+        out_ref[:, h * 512 : h * 512 + 512] = parts[h].astype(jnp.bfloat16)
 
     for copy in sends:
         copy.wait_send()
@@ -548,12 +567,13 @@
     return pl.pallas_call(
         kernel,
         out_shape=jax.ShapeDtypeStruct((NO, 1024), bf),
-        in_specs=[anywhere, vm, anywhere, smem, smem, smem],
+        in_specs=[anywhere, anywhere, anywhere, smem, smem, smem],
         out_specs=vm,
         scratch_shapes=[
             pltpu.VMEM((32, 16, KK), bf),
             pltpu.VMEM((NY, 32, PIECE), bf),
-            pltpu.VMEM((NY, NX, 32, PIECE), bf),
+            pltpu.VMEM((NX, 32, PIECE), bf),
+            pltpu.VMEM((NY, 32, NX * CW * DW), bf),
             pltpu.VMEM((256, KK), bf),
             pltpu.VMEM((CW, NO, 512), bf),
             pltpu.VMEM((4, 256, 128), f32),
@@ -563,6 +583,7 @@
             pltpu.VMEM((256, 256), bf),
             pltpu.VMEM((1024, 128), bf),
             pltpu.VMEM((CW, 16, 128), bf),
+            pltpu.VMEM((16, CW, 4, DW), bf),
             pltpu.VMEM((64, PIECE), bf),
             pltpu.VMEM((16, CW, SA, NO), bf),
             pltpu.VMEM((512, 256), f32),
@@ -570,7 +591,7 @@
             pltpu.VMEM((1024, 128), f32),
             pltpu.VMEM((512, 256), bf),
             pltpu.VMEM((4, 128, 256), bf),
-            dma((96,)), dma((96,)), dma((4,)), dma, dma, dma((3,)), dma((3,)), dma,
+            dma((96,)), dma((96,)), dma((5,)), dma, dma, dma((3,)), dma((3,)), dma((4,)),
         ],
         compiler_params=pltpu.CompilerParams(
             collective_id=0, has_side_effects=True, vmem_limit_bytes=64 * 1024 * 1024
@@ -581,8 +602,7 @@
 
 def local(amplitudes, integrals, hole_integrals, irreps, occ_energy, vir_energy):
     t = jnp.transpose(amplitudes.reshape(8, 16, CW, NV), (0, 2, 1, 3))
-    vv = jnp.transpose(integrals, (1, 0, 2, 3)).reshape(64, CW, DW)
-    vv = jnp.pad(vv, ((0, 0), (0, 0), (0, 256 - DW))).reshape(64, PIECE)
+    vv = jnp.transpose(integrals, (0, 2, 1, 3))
     w = jnp.transpose(hole_integrals.reshape(NO, 16, CW, SA), (1, 2, 3, 0))
     out = call(t, vv, w, irreps, occ_energy, vir_energy)
     return out.reshape(8, 1, 1, 1, 16, 16, SA)

time: 78.5 us -> 76.9 us (0.980)
  local copies, waits for them, and re-layouts: 3.84 us -> 2.13 us
    unnamed x3 -> x0, local copies, waits for them, and re-layouts: 1.64 us -> none
where the time goes in v4:
time: 76.9 us; the launch traced here: 76.2 us
  Pallas kernels  74 us (96%)
  local copies, waits for them, and re-layouts  2.13 us (3%)
    pallas_call x1, Pallas kernels, call(): pl.pallas_call(kernel, out_shape=jax.ShapeDtypeStruct((NO, 1024), bf), in...  74 us
    reshape x1, local copies, waits for them, and re-layouts, local(): return out.reshape(8, 1, 1, 1, 16, 16, SA)  2.13 us

profile of v4, /device:TPU:1, one launch (start us, length us, event | category | flops | bytes accessed | tf_op | source)
XLA Modules:
  0.0 76.2 jit_solution(12335472908999174633)
XLA Ops:
  0.0 74.0 %shard_map.64 = bf16[128,1024]{1,0:T(8,128)(2,1)} custom-call(bf16[8,3,16,1792]{3,2,1,0:T(8,128)(2,1)} %bitcast.8, bf16[16,3,4,224]{3,2,1,0:T(4,128)(2,1)} %bitcast.10, bf16[16,3,64,128]{3,2,1,0:T(8,128)(2,1)} %bitcast.9, s32[112]{0:T(128)} %irreps.1, f32[128]{0:T(128)} %occ.1, f32[64]{0:T(128)} %vir.1), custom_call_target="tpu_custom_call" | custom-call | flops 1409286144 | bytes 20000000 | tf_op jit(solution)/shard_map/pallas_call | solution.py:567
  74.0 2.1 %reshape.11 = bf16[8,1,1,1,16,16,64]{6,5,4,0,3,2,1:T(8,128)(2,1)} reshape(bf16[128,1024]{1,0:T(8,128)(2,1)} %shard_map.64) | data formatting | bytes 524288 | tf_op jit(solution)/shard_map/reshape | solution.py:608

commit v5 on v4

--- a/solution.py
+++ b/solution.py
@@ -88,11 +88,8 @@
     for n in range(1, NX):
         greet(dev(lax.rem(x + n, NX), y, z, k))
 
-    def greet_y(n, carry):
-        greet(dev(x, lax.rem(y + n, NY), z, k))
-        return carry
-
-    lax.fori_loop(1, NY, greet_y, 0)
+    for d in range(2):
+        greet(dev(x, ys[d], z, k))
 
     def greet_z(n, carry):
         other = lax.rem(z * 2 + k + n, 16)
@@ -107,12 +104,6 @@
         far = jnp.where(lax.rem(m, 2) == 1, 4 - lax.div(m + 1, 2), 4 + lax.div(m, 2))
         return (lax.rem(x + 3 - lax.rem(n, NX), NX), lax.rem(y + far, NY))
 
-    def greet_mail(n, carry):
-        px, py = partner(n)
-        greet(dev(px, py, z, twin))
-        return carry
-
-    lax.fori_loop(0, 32 - first, greet_mail, 0)
     label = jnp.bitwise_xor(jnp.bitwise_xor(irreps[v], irreps[zl]), irreps[0])
     lane = lax.broadcasted_iota(jnp.int32, (8, PIECE), 1) & 255
     kept = jnp.zeros((8, PIECE), jnp.float32)
@@ -140,7 +131,7 @@
         axis=0,
     )
     a_own[...] = dot(wide, pull[...]).astype(jnp.bfloat16).reshape(CW, 16, 128)
-    pl.semaphore_wait(barrier, 3 + 7 + 15 + 32 - first)
+    pl.semaphore_wait(barrier, 3 + 2 + 15)
 
     names = {}
     sends = []
@@ -256,8 +247,6 @@
         def _():
             remote(a_own, slab_place(block), a_send, a_recv, dev(x, y, az, ak)).start()
 
-    t_start(0)
-    t_start(1)
     for src, dst, n in raw:
         pltpu.make_async_copy(src, dst, rsem.at[n]).wait()
         if n == raw[0][2]:
@@ -265,6 +254,8 @@
             go(v0_y(1, 0))
     for n in range(1, NX):
         go(v1_x(n))
+    t_start(0)
+    t_start(1)
 
     def v0_step(s):
         v0_y(0, s).wait_recv()
@@ -345,6 +336,97 @@
     go(v0_x(0, 1))
     go(v0_x(1, 0))
     slab_step(0)
+    v1_step(1)
+    slab_step(1)
+    v0_x(0, 0).wait_recv()
+    go(v0_f(0))
+    v0_x(1, 1).wait_recv()
+    go(v0_f(1))
+    slab_step(2)
+    t_step(2)
+    v1_step(2)
+    slab_step(3)
+    w_load.wait()
+    zmat = None
+    for c in range(CW):
+        rows = w_own[:, c, pl.ds(pl.multiple_of(blk_b * 16, 16), 16), :].reshape(256, NO)
+        part = dot(rows, a_mat[c])
+        zmat = part if zmat is None else zmat + part
+    for block in range(4):
+        zs[block] = zmat[:, block * 128 : block * 128 + 128]
+    chunk = lax.broadcasted_iota(jnp.int32, (16, 128), 1) >> 4
+
+    def crossed(block, carry):
+        for h in range(2):
+            outs = [jnp.zeros((16, 128), jnp.float32)] * 8
+            for b in range(8):
+                part = zs[block, pl.ds(h * 8 + b, 16, stride=16), :]
+                for q in range(8):
+                    moved = pltpu.roll(part, (b - q) % 8 * 16, 1) if b != q else part
+                    outs[q] = jnp.where(chunk == b, -moved, outs[q])
+            for q in range(8):
+                acc[h, pl.ds(pl.multiple_of(block * 128 + q * 16, 16), 16), :] = outs[q]
+        return carry
+
+    lax.fori_loop(0, 4, crossed, 0)
+
+    t_step(3)
+    t_last(0)
+    v0_x(0, 1).wait_recv()
+    v0_x(1, 0).wait_recv()
+    for d in range(2):
+        v0_f(d).wait_recv()
+    join1(near_half)
+    for u in range(4):
+        t_sibling(1, u).wait_recv()
+    ladder(0, near_half)
+    v1_step(3)
+    join1(1 - near_half)
+    def near(n):
+        return lax.rem(zl + ABOVE[n], NZL)
+
+    def tile_row(si, sj, h):
+        return (si // 2 * 2 + sj // 2) * 8 + (si % 2 * 2 + sj % 2) * 2 + h
+
+    def fill(pair, half):
+        for si in (2 * pair, 2 * pair + 1):
+            for sj in (2 * half, 2 * half + 1):
+                for xj in range(4):
+                    for h in range(2):
+                        mail[pl.ds(xj * 256 + tile_row(si, sj, h), 8, stride=32), :] = acc[
+                            h, pl.ds(si * 128 + near(sj) * 4 + xj, 8, stride=16), :
+                        ]
+
+    def post(part, start, rows):
+        def send_mail(n, carry):
+            px, py = partner(n)
+            src = mail.at[pl.ds(pl.multiple_of((px * 8 + py) * 32 + start, 8), rows)]
+            dst = rec.at[pl.ds(pl.multiple_of((x * 8 + y) * 32 + start, 8), rows)]
+            remote(src, dst, m_send.at[part], m_recv.at[part], dev(px, py, z, twin)).start()
+            return carry
+
+        lax.fori_loop(0, 32 - first, send_mail, 0)
+
+        @pl.when(diag)
+        def _():
+            here = pl.ds(pl.multiple_of((x * 8 + y) * 32 + start, 8), rows)
+            pltpu.make_async_copy(mail.at[here], rec.at[here], m_recv.at[part]).start()
+
+    ladder(0, 1 - near_half)
+    fill(0, 0)
+    fill(0, 1)
+    post(0, 0, 16)
+    t_last(1)
+    for block in (2, 3):
+        for u in range(4):
+            t_sibling(block, u).wait_recv()
+    for half in range(2):
+        ladder(1, half)
+    fill(1, 0)
+    post(1, 16, 8)
+    fill(1, 1)
+    post(2, 24, 8)
+
     m = lax.broadcasted_iota(jnp.int32, (256, 256), 0)
     n = lax.broadcasted_iota(jnp.int32, (256, 256), 1)
     hit = jnp.logical_and(m >> 4 == (n & 15), (m & 15) == n >> 4)
@@ -362,102 +444,11 @@
         for q in range(8):
             e_i = occ[q * 16 + lax.rem(zl + ABOVE[block], NZL) * 4 + x]
             denom[block * 128 + q * 16 : block * 128 + q * 16 + 16, :] = ((e_i + e_j) - e_a) - e_b
-    v1_step(1)
-    slab_step(1)
     m = lax.broadcasted_iota(jnp.int32, (512, 512), 0)
     n = lax.broadcasted_iota(jnp.int32, (512, 512), 1)
     hit = jnp.logical_and((m >> 4 & 7) == n >> 6, m >> 7 == (n >> 4 & 3))
     hit = jnp.logical_and(hit, (m & 15) == (n & 15))
     order[...] = jnp.where(hit, 1.0, 0.0).astype(jnp.bfloat16)
-
-    v0_x(0, 0).wait_recv()
-    go(v0_f(0))
-    v0_x(1, 1).wait_recv()
-    go(v0_f(1))
-    slab_step(2)
-    t_step(2)
-    v1_step(2)
-    slab_step(3)
-    w_load.wait()
-    zmat = None
-    for c in range(CW):
-        rows = w_own[:, c, pl.ds(pl.multiple_of(blk_b * 16, 16), 16), :].reshape(256, NO)
-        part = dot(rows, a_mat[c])
-        zmat = part if zmat is None else zmat + part
-    for block in range(4):
-        zs[block] = zmat[:, block * 128 : block * 128 + 128]
-    chunk = lax.broadcasted_iota(jnp.int32, (16, 128), 1) >> 4
-
-    def crossed(block, carry):
-        for h in range(2):
-            outs = [jnp.zeros((16, 128), jnp.float32)] * 8
-            for b in range(8):
-                part = zs[block, pl.ds(h * 8 + b, 16, stride=16), :]
-                for q in range(8):
-                    moved = pltpu.roll(part, (b - q) % 8 * 16, 1) if b != q else part
-                    outs[q] = jnp.where(chunk == b, -moved, outs[q])
-            for q in range(8):
-                acc[h, pl.ds(pl.multiple_of(block * 128 + q * 16, 16), 16), :] = outs[q]
-        return carry
-
-    lax.fori_loop(0, 4, crossed, 0)
-
-    t_step(3)
-    t_last(0)
-    v0_x(0, 1).wait_recv()
-    v0_x(1, 0).wait_recv()
-    for d in range(2):
-        v0_f(d).wait_recv()
-    join1(near_half)
-    for u in range(4):
-        t_sibling(1, u).wait_recv()
-    ladder(0, near_half)
-    v1_step(3)
-    join1(1 - near_half)
-    def near(n):
-        return lax.rem(zl + ABOVE[n], NZL)
-
-    def tile_row(si, sj, h):
-        return (si // 2 * 2 + sj // 2) * 8 + (si % 2 * 2 + sj % 2) * 2 + h
-
-    def fill(pair, half):
-        for si in (2 * pair, 2 * pair + 1):
-            for sj in (2 * half, 2 * half + 1):
-                for xj in range(4):
-                    for h in range(2):
-                        mail[pl.ds(xj * 256 + tile_row(si, sj, h), 8, stride=32), :] = acc[
-                            h, pl.ds(si * 128 + near(sj) * 4 + xj, 8, stride=16), :
-                        ]
-
-    def post(part, start, rows):
-        def send_mail(n, carry):
-            px, py = partner(n)
-            src = mail.at[pl.ds(pl.multiple_of((px * 8 + py) * 32 + start, 8), rows)]
-            dst = rec.at[pl.ds(pl.multiple_of((x * 8 + y) * 32 + start, 8), rows)]
-            remote(src, dst, m_send.at[part], m_recv.at[part], dev(px, py, z, twin)).start()
-            return carry
-
-        lax.fori_loop(0, 32 - first, send_mail, 0)
-
-        @pl.when(diag)
-        def _():
-            here = pl.ds(pl.multiple_of((x * 8 + y) * 32 + start, 8), rows)
-            pltpu.make_async_copy(mail.at[here], rec.at[here], m_recv.at[part]).start()
-
-    ladder(0, 1 - near_half)
-    fill(0, 0)
-    fill(0, 1)
-    post(0, 0, 16)
-    t_last(1)
-    for block in (2, 3):
-        for u in range(4):
-            t_sibling(block, u).wait_recv()
-    for half in range(2):
-        ladder(1, half)
-    fill(1, 0)
-    post(1, 16, 8)
-    fill(1, 1)
-    post(2, 24, 8)
 
     owner_z = lax.div(blk_a, 2) * NZL
     owner_k = lax.rem(blk_a, 2)

time: 76.9 us -> 75.1 us (0.977)
  Pallas kernels: 74 us -> 72.8 us
    pallas_call x1, Pallas kernels: 74 us -> 72.8 us  [call(): pl.pallas_call(kernel, out_shape=jax.ShapeDtypeStruct((NO, 1024), bf), in...]
where the time goes in v5:
time: 75.1 us; the launch traced here: 75 us
  Pallas kernels  72.8 us (97%)
  local copies, waits for them, and re-layouts  2.13 us (3%)
    pallas_call x1, Pallas kernels, call(): pl.pallas_call(kernel, out_shape=jax.ShapeDtypeStruct((NO, 1024), bf), in...  72.8 us
    reshape x1, local copies, waits for them, and re-layouts, local(): return out.reshape(8, 1, 1, 1, 16, 16, SA)  2.13 us

profile of v5, /device:TPU:1, one launch (start us, length us, event | category | flops | bytes accessed | tf_op | source)
XLA Modules:
  0.0 75.0 jit_solution(2693584475718449137)
XLA Ops:
  0.0 72.8 %shard_map.64 = bf16[128,1024]{1,0:T(8,128)(2,1)} custom-call(bf16[8,3,16,1792]{3,2,1,0:T(8,128)(2,1)} %bitcast.8, bf16[16,3,4,224]{3,2,1,0:T(4,128)(2,1)} %bitcast.10, bf16[16,3,64,128]{3,2,1,0:T(8,128)(2,1)} %bitcast.9, s32[112]{0:T(128)} %irreps.1, f32[128]{0:T(128)} %occ.1, f32[64]{0:T(128)} %vir.1), custom_call_target="tpu_custom_call" | custom-call | flops 1409286144 | bytes 20000000 | tf_op jit(solution)/shard_map/pallas_call | solution.py:558
  72.8 2.1 %reshape.11 = bf16[8,1,1,1,16,16,64]{6,5,4,0,3,2,1:T(8,128)(2,1)} reshape(bf16[128,1024]{1,0:T(8,128)(2,1)} %shard_map.64) | data formatting | bytes 524288 | tf_op jit(solution)/shard_map/reshape | solution.py:599

commit v6 on v5

--- a/solution.py
+++ b/solution.py
@@ -353,7 +353,7 @@
         part = dot(rows, a_mat[c])
         zmat = part if zmat is None else zmat + part
     for block in range(4):
-        zs[block] = zmat[:, block * 128 : block * 128 + 128]
+        zs[block, 0:256, :] = zmat[:, block * 128 : block * 128 + 128]
     chunk = lax.broadcasted_iota(jnp.int32, (16, 128), 1) >> 4
 
     def crossed(block, carry):
@@ -567,9 +567,9 @@
             pltpu.VMEM((NY, 32, NX * CW * DW), bf),
             pltpu.VMEM((256, KK), bf),
             pltpu.VMEM((CW, NO, 512), bf),
-            pltpu.VMEM((4, 256, 128), f32),
-            pltpu.VMEM((2, 512, 128), f32),
-            pltpu.VMEM((2, 512, 128), f32),
+            pltpu.VMEM((4, 288, 128), f32),
+            pltpu.VMEM((2, 528, 128), f32),
+            pltpu.VMEM((2, 528, 128), f32),
             pltpu.VMEM((512, 512), bf),
             pltpu.VMEM((256, 256), bf),
             pltpu.VMEM((1024, 128), bf),
@@ -578,8 +578,8 @@
             pltpu.VMEM((64, PIECE), bf),
             pltpu.VMEM((16, CW, SA, NO), bf),
             pltpu.VMEM((512, 256), f32),
-            pltpu.VMEM((1024, 128), f32),
-            pltpu.VMEM((1024, 128), f32),
+            pltpu.VMEM((1056, 128), f32),
+            pltpu.VMEM((1056, 128), f32),
             pltpu.VMEM((512, 256), bf),
             pltpu.VMEM((4, 128, 256), bf),
             dma((96,)), dma((96,)), dma((5,)), dma, dma, dma((3,)), dma((3,)), dma((4,)),

time: 75.1 us -> 75.1 us (level)
  no operation moved by 1% of the time
where the time goes in v6:
time: 75.1 us; the launch traced here: 75 us
  Pallas kernels  72.8 us (97%)
  local copies, waits for them, and re-layouts  2.13 us (3%)
    pallas_call x1, Pallas kernels, call(): pl.pallas_call(kernel, out_shape=jax.ShapeDtypeStruct((NO, 1024), bf), in...  72.8 us
    reshape x1, local copies, waits for them, and re-layouts, local(): return out.reshape(8, 1, 1, 1, 16, 16, SA)  2.13 us

profile of v6, /device:TPU:1, one launch (start us, length us, event | category | flops | bytes accessed | tf_op | source)
XLA Modules:
  0.0 75.0 jit_solution(5180188685265600971)
XLA Ops:
  0.0 72.8 %shard_map.64 = bf16[128,1024]{1,0:T(8,128)(2,1)} custom-call(bf16[8,3,16,1792]{3,2,1,0:T(8,128)(2,1)} %bitcast.8, bf16[16,3,4,224]{3,2,1,0:T(4,128)(2,1)} %bitcast.10, bf16[16,3,64,128]{3,2,1,0:T(8,128)(2,1)} %bitcast.9, s32[112]{0:T(128)} %irreps.1, f32[128]{0:T(128)} %occ.1, f32[64]{0:T(128)} %vir.1), custom_call_target="tpu_custom_call" | custom-call | flops 1409286144 | bytes 20000000 | tf_op jit(solution)/shard_map/pallas_call | solution.py:558
  72.8 2.1 %reshape.11 = bf16[8,1,1,1,16,16,64]{6,5,4,0,3,2,1:T(8,128)(2,1)} reshape(bf16[128,1024]{1,0:T(8,128)(2,1)} %shard_map.64) | data formatting | bytes 524288 | tf_op jit(solution)/shard_map/reshape | solution.py:599
